TPU v7x, 32 devices: a whole 2x2x4 slice. The times are simulated.
32 devices in a mesh: group: 2 (over y), row: 16 (over z, x, core).
Axes of the slice: x: 2, y: 2, z: 4, core: 2. Of those that a mesh axis runs over, the one named last changes fastest.
Arguments:
- image: bfloat16 [128, 256, 256], P(('group', 'row')), parts along dimension 0, may hold values from -6 to 6
- tissue: int32 [32, 2], P(('group', 'row')), parts along dimension 0, may hold values from 0 to 1, as said below
- kernel: float32 [7, 7, 256], replicated, may hold values from -0.875 to 0.875
- ln_gain: float32 [256], replicated, may hold values from 0.5 to 1.5
- w_in: bfloat16 [256, 1024], replicated, may hold values from -0.375 to 0.375
- w_out: bfloat16 [1024, 256], replicated, may hold values from -0.1875 to 0.1875
- layer_scale: float32 [256], replicated, may hold values from 0.5 to 1.5
- cotangent: bfloat16 [128, 256, 256], P(('group', 'row')), parts along dimension 0, may hold values from -6 to 6
Outputs:
- block_out: bfloat16 [128, 256, 256], P(('group', 'row')), parts along dimension 0
- grad_image: bfloat16 [128, 256, 256], P(('group', 'row')), parts along dimension 0
- grad_w_in: float32 [512, 1024], P(('group', 'row')), parts along dimension 0
- grad_w_out: float32 [2048, 256], P(('group', 'row')), parts along dimension 0
- small_grads: float32 [102, 256], P('group'), parts along dimension 0
There are 2 independent parts, one for each index of `group`. A program takes and returns all parts, laid end to end along the dimension named above; an argument that names none is the same for every part. Nothing has to cross between parts.
Inputs may be any that keep to these rules, and one draw needn't show every extreme that they name: 1 marks a tile of 4 x 128 positions that holds tissue, 0 one without. Among the 2 tiles of the 4 rows of one device, at least one is 0 and at least one is 1.
All inputs are finite; a program needn't handle non-finite values.
Results may differ from a plain program's by a relative error of at most 0.0063.
Values may be sent and summed in bfloat16 or wider, within the bound.
A program may use at most 64 MiB of HBM per device.

v0:
```python
import jax
import jax.numpy as jnp
from jax import lax
from jax.sharding import PartitionSpec as P

KERNEL = 7
TILE_ROWS = 4
TILE_COLS = 128


EPSILON = 1e-06
ROOT_TWO_PI = 0.7978845608028654
CUBIC_TERM = 0.044715


def padded_2(block, sides, width):
    for axis, dim in sides:
        count = lax.axis_size(axis)
        forward = [(i, i + 1) for i in range(count - 1)]
        backward = [(target, source) for source, target in forward]
        low = lax.ppermute(
            lax.slice_in_dim(block, block.shape[dim] - width, None, axis=dim), axis, forward
        )
        high = lax.ppermute(lax.slice_in_dim(block, 0, width, axis=dim), axis, backward)
        block = jnp.concatenate([low, block, high], axis=dim)
    return block


def gelu_value(inputs):
    tangent = jnp.tanh(ROOT_TWO_PI * (inputs + CUBIC_TERM * inputs * inputs * inputs))
    return 0.5 * inputs * (1.0 + tangent)


def gelu_slope(inputs):
    tangent = jnp.tanh(ROOT_TWO_PI * (inputs + CUBIC_TERM * inputs * inputs * inputs))
    return 0.5 * (1.0 + tangent) + 0.5 * inputs * (1.0 - tangent * tangent) * ROOT_TWO_PI * (
        1.0 + 3.0 * CUBIC_TERM * inputs * inputs
    )


def depthwise(padded, kernel, image_rows, image_cols):
    total = jnp.zeros((image_rows, image_cols, kernel.shape[-1]), jnp.float32)
    for row_tap in range(KERNEL):
        for col_tap in range(KERNEL):
            total = (
                total
                + padded[row_tap : row_tap + image_rows, col_tap : col_tap + image_cols]
                * kernel[row_tap, col_tap]
            )
    return total


def kernel_terms(padded, grads, image_rows, image_cols):
    collected = []
    for row_tap in range(KERNEL):
        for col_tap in range(KERNEL):
            collected.append(
                jnp.sum(
                    padded[row_tap : row_tap + image_rows, col_tap : col_tap + image_cols] * grads,
                    axis=(0, 1),
                )
            )
    return jnp.stack(collected)


def shards(image, tissue, kernel, ln_gain, w_in, w_out, layer_scale, cotangent):
    half_width = KERNEL // 2
    image_rows, image_cols, channels = image.shape
    hidden = w_in.shape[1]
    tile_size = TILE_ROWS * TILE_COLS

    def to_tiles(values):
        depth_last = values.shape[-1]
        values = values.reshape(
            image_rows // TILE_ROWS, TILE_ROWS, image_cols // TILE_COLS, TILE_COLS, depth_last
        )
        return values.transpose(0, 2, 1, 3, 4).reshape(-1, tile_size, depth_last)

    def from_tiles(values):
        depth_last = values.shape[-1]
        values = values.reshape(
            image_rows // TILE_ROWS, image_cols // TILE_COLS, TILE_ROWS, TILE_COLS, depth_last
        )
        return values.transpose(0, 2, 1, 3, 4).reshape(image_rows, image_cols, depth_last)

    extended = padded_2(image, (("row", 0),), half_width)
    padded = jnp.pad(extended.astype(jnp.float32), ((0, 0), (half_width, half_width), (0, 0)))
    filtered = depthwise(padded, kernel, image_rows, image_cols)
    centre = jnp.mean(filtered, axis=-1, keepdims=True)
    centered = filtered - centre
    inv_std = lax.rsqrt(jnp.mean(centered * centered, axis=-1, keepdims=True) + EPSILON)
    standard = centered * inv_std
    normed = (standard * ln_gain).astype(jnp.bfloat16)
    tissue_at = jnp.repeat(jnp.repeat(tissue, TILE_ROWS, axis=0), TILE_COLS, axis=1).astype(
        jnp.float32
    )[:, :, None]
    upstream = cotangent.astype(jnp.float32)
    grad_out = (tissue_at * layer_scale * upstream).astype(jnp.bfloat16)
    normed_tiles = to_tiles(normed)
    grad_tiles = to_tiles(grad_out)
    has_tissue = tissue.reshape(-1)

    def tile_work(normed_blk, grad_blk):
        pre_act = jnp.dot(normed_blk, w_in, preferred_element_type=jnp.float32)
        activation = gelu_value(pre_act).astype(jnp.bfloat16)
        branch = jnp.dot(activation, w_out, preferred_element_type=jnp.float32)
        grad_act = jnp.dot(grad_blk, w_out.T, preferred_element_type=jnp.float32)
        grad_pre = (grad_act * gelu_slope(pre_act)).astype(jnp.bfloat16)
        grad_norm = jnp.dot(grad_pre, w_in.T, preferred_element_type=jnp.float32)
        return (activation, branch, grad_pre, grad_norm)

    def per_tile(record):
        return tile_work(record[0], record[1])

    act_tiles, branch_tiles, pre_tiles, norm_tiles = lax.map(
        per_tile, (normed_tiles, grad_tiles, has_tissue)
    )
    normed_flat = normed_tiles.reshape(-1, channels)
    grad_flat = grad_tiles.reshape(-1, channels)
    act_flat = act_tiles.reshape(-1, hidden)
    pre_flat = pre_tiles.reshape(-1, hidden)
    section = normed_flat
    grad_w_in = lax.psum_scatter(
        lax.dot_general(
            section, pre_flat, (((0,), (0,)), ((), ())), preferred_element_type=jnp.float32
        ),
        "row",
        scatter_dimension=0,
        tiled=True,
    )
    section = act_flat
    grad_w_out = lax.psum_scatter(
        lax.dot_general(
            section, grad_flat, (((0,), (0,)), ((), ())), preferred_element_type=jnp.float32
        ),
        "row",
        scatter_dimension=0,
        tiled=True,
    )
    branch = from_tiles(branch_tiles)
    grad_norm = from_tiles(norm_tiles)
    block_out = (image.astype(jnp.float32) + tissue_at * layer_scale * branch).astype(jnp.bfloat16)
    scale_grad = jnp.sum(tissue_at * branch * upstream, axis=(0, 1))
    gain_grad = jnp.sum(grad_norm * standard, axis=(0, 1))
    grad_std = grad_norm * ln_gain
    grad_conv = (
        inv_std
        * (
            grad_std
            - jnp.mean(grad_std, axis=-1, keepdims=True)
            - standard * jnp.mean(grad_std * standard, axis=-1, keepdims=True)
        )
    ).astype(jnp.bfloat16)
    grad_float = grad_conv.astype(jnp.float32)
    kernel_grad = kernel_terms(padded, grad_float, image_rows, image_cols)
    packed = jnp.concatenate([kernel_grad, gain_grad[None], scale_grad[None]], axis=0)
    small_grads = lax.psum(packed, "row")
    grad_ext = padded_2(grad_conv, (("row", 0),), half_width)
    grad_padded = jnp.pad(grad_ext.astype(jnp.float32), ((0, 0), (half_width, half_width), (0, 0)))
    conv_back = depthwise(grad_padded, kernel[::-1, ::-1], image_rows, image_cols)
    grad_image = (upstream + conv_back).astype(jnp.bfloat16)
    return (block_out, grad_image, grad_w_in, grad_w_out, small_grads)


def solution(mesh):
    placed = (
        P(("group", "row"), None, None),
        P(("group", "row"), None),
        P(),
        P(),
        P(),
        P(),
        P(),
        P(("group", "row"), None, None),
    )
    return jax.shard_map(
        shards,
        mesh=mesh,
        in_specs=placed,
        out_specs=(
            P(("group", "row"), None, None),
            P(("group", "row"), None, None),
            P(("group", "row"), None),
            P(("group", "row"), None),
            P("group", None),
        ),
        check_vma=False,
    )
```

profile of v0, /device:TPU:0, one launch (start us, length us, event | category | flops | bytes accessed | tf_op | source)
XLA Modules:
  0.0 192.2 jit_solution(3248807306275557346)
XLA Ops:
  7.2 1.2 fusion.134
  8.5 2.4 %collective-permute-start = (bf16[3,256,256]{2,1,0:T(8,128)(2,1)S(1)}, bf16[3,256,256]{2,1,0:T(8,128)(2,1)S(1)}, u32[]{:S(2)}, u32[]{:S(2)}) collective-permute-start(bf16[3,256,256]{2,1,0:T(8,128)(2,1)S(1)} %get-tuple-element.138), channel_id=1, source_target_pairs={{0,1},{1,2},{2,3},{3,4},{4,5},{5,6},{6,7},{7,8},{8,9},{9,10},{10,1... | collective-permute-start | bytes 1179656 | tf_op jit(solution)/shard_map/ppermute | solution.py:21
  10.8 1.3 collective-permute-start.1
  12.9 1.6 fusion.135
  14.5 1.2 fusion.18
  17.9 1.2 maximum_convert_fusion
  19.1 10.2 %fusion.132 = (f32[4,256]{1,0:T(4,128)S(1)}, f32[4,256,256]{2,1,0:T(8,128)}) fusion(f32[256]{0:T(256)} %bitcast.255, f32[256]{0:T(256)} %bitcast.257, f32[256]{0:T(256)S(1)} %bitcast.201, f32[256]{0:T(256)S(1)} %bitcast.203, f32[10,256,256]{2,1,0:T(8,128)S(1)} %maximum_convert_fusion, f32[256]{0:T(256)S(1)} %bitcast.205, f32[256]{0:T(256)} %bitcast.207, ...), kind=kLoop, calls=%fused_computation.229 | loop fusion | flops 25689088 | bytes 11064320 | tf_op jit(solution)/shard_map/reduce_sum | solution.py:89
  29.3 1.7 multiply_reduce_fusion.2
  31.0 1.6 multiply_convert_fusion.3
  33.4 16.7 %while.16 = (s32[]{:T(128)}, bf16[2,512,1024]{2,1,0:T(8,128)(2,1)}, f32[2,512,256]{2,1,0:T(8,128)}, bf16[2,512,1024]{2,1,0:T(8,128)(2,1)}, f32[2,512,256]{2,1,0:...) while((s32[]{:T(128)}, bf16[2,512,1024]{2,1,0:T(8,128)(2,1)}, ...), condition=%wide.region_3.4_spmd, body=%wide.region_2.3_spmd.sunk | while | flops 1093140480 | bytes 51906900 | solution.py:115
  33.4 2.9 %bitcast_dynamic-update-slice_fusion.4 = (bf16[2,512,1024]{2,1,0:T(8,128)(2,1)}, f32[512,1024]{1,0:T(8,128)S(1)}) fusion(bf16[2,512,1024]{2,1,0:T(8,128)(2,1)} %get-tuple-element.263, s32[]{:T(128)S(6)} %copy.42, bf16[256,1024]{1,0:T(8,128)(2,1)S(1)} %get-tuple-element.278, bf16[2,512,256]{2,1,0:T(8,128)(2,1)} %get-tuple-element.277), kind=kOutput, calls=%fused_computation.15.clone.1 | convolution fusion | flops 273154048 | bytes 3933184 | tf_op jit(solution)/shard_map/while/body/eval_jaxpr/dot_general | solution.py:104
  37.9 1.4 bitcast_dynamic-update-slice_fusion.5
  40.7 1.0 copy-done.6
  41.7 2.9 %bitcast_dynamic-update-slice_fusion.4 = (bf16[2,512,1024]{2,1,0:T(8,128)(2,1)}, f32[512,1024]{1,0:T(8,128)S(1)}) fusion(bf16[2,512,1024]{2,1,0:T(8,128)(2,1)} %get-tuple-element.263, s32[]{:T(128)S(6)} %copy.42, bf16[256,1024]{1,0:T(8,128)(2,1)S(1)} %get-tuple-element.278, bf16[2,512,256]{2,1,0:T(8,128)(2,1)} %get-tuple-element.277), kind=kOutput, calls=%fused_computation.15.clone.1 | convolution fusion | flops 273154048 | bytes 3933184 | tf_op jit(solution)/shard_map/while/body/eval_jaxpr/dot_general | solution.py:104
  46.3 1.4 bitcast_dynamic-update-slice_fusion.5
  50.1 1.5 fusion.116
  51.6 1.3 copy.26
  53.8 2.3 %fusion.65 = (f32[256]{0:T(256)}, f32[256]{0:T(256)}, f32[256]{0:T(256)}, f32[256]{0:T(256)}, f32[256]{0:T(256)}, /*index=5*/f32[256]{0:T(256)}, f32[256]{0:T(25...) fusion(f32[10,256,256]{2,1,0:T(8,128)S(1)} %maximum_convert_fusion, f32[4,256]{1,0:T(4,128)S(1)} %broadcast_multiply_fusion, ...), kind=kLoop, calls=%fused_computation.127 | loop fusion | flops 7075584 | bytes 6318080 | tf_op jit(solution)/shard_map/reduce_sum | solution.py:58
  56.1 1.9 fusion.67
  58.8 1.7 fusion.139
  60.6 7.4 %collective-permute-start.2 = (bf16[3,256,256]{2,1,0:T(8,128)(2,1)}, bf16[3,256,256]{2,1,0:T(8,128)(2,1)}, u32[]{:S(2)}, u32[]{:S(2)}) collective-permute-start(bf16[3,256,256]{2,1,0:T(8,128)(2,1)} %get-tuple-element.136), channel_id=1, source_target_pairs={{0,1},{1,2},{2,3},{3,4},{4,5},{5,6},{6,7},{7,8},{8,9},{9,10},{10,1... | collective-permute-start | bytes 1179656 | tf_op jit(solution)/shard_map/ppermute | solution.py:21
  68.0 1.5 collective-permute-start.3
  69.5 3.5 %fusion.138 = f32[256,1024]{1,0:T(8,128)} fusion(bf16[1024,256]{1,0:T(8,128)(2,1)} %bitcast.192, bf16[1024,1024]{1,0:T(8,128)(2,1)} %bitcast.190), kind=kOutput, calls=%fused_computation.235 | convolution fusion | flops 536870912 | bytes 3670016 | tf_op jit(solution)/shard_map/dot_general | solution.py:124
  73.0 1.9 %fusion.68 = (f32[256]{0:T(256)}, f32[256]{0:T(256)}, f32[256]{0:T(256)}, f32[256]{0:T(256)}, f32[256]{0:T(256)}, /*index=5*/f32[256]{0:T(256)}, f32[256]{0:T(256)}, f32[256]{0:T(256)}, f32[256]{0:T(256)}, f32[256]{0:T(256)}) fusion(bf16[4,256,256]{2,1,0:T(8,128)(2,1)S(1)} %get-tuple-element.127, f32[10,256,256]{2,1,0:T(8,128)S(1)} %maximum_convert_fusion), kind=kLoop, calls=%fused_computation.130 | loop fusion | flops 5502464 | bytes 5253120 | tf_op jit(solution)/shard_map/reduce_sum | solution.py:58
  75.0 1.9 %fusion.69 = (f32[256]{0:T(256)}, f32[256]{0:T(256)}, f32[256]{0:T(256)}, f32[256]{0:T(256)}, f32[256]{0:T(256)}, /*index=5*/f32[256]{0:T(256)}, f32[256]{0:T(256)}, f32[256]{0:T(256)}, f32[256]{0:T(256)}, f32[256]{0:T(256)}) fusion(bf16[4,256,256]{2,1,0:T(8,128)(2,1)S(1)} %get-tuple-element.127, f32[10,256,256]{2,1,0:T(8,128)S(1)} %maximum_convert_fusion), kind=kLoop, calls=%fused_computation.131 | loop fusion | flops 5502464 | bytes 5253120 | tf_op jit(solution)/shard_map/reduce_sum | solution.py:58
  76.9 2.0 %fusion.66 = (f32[256]{0:T(256)}, f32[256]{0:T(256)}, f32[256]{0:T(256)}, f32[256]{0:T(256)}, f32[256]{0:T(256)}, /*index=5*/f32[256]{0:T(256)}, f32[256]{0:T(256)}, f32[256]{0:T(256)}, f32[256]{0:T(256)}, f32[256]{0:T(256)}) fusion(bf16[4,256,256]{2,1,0:T(8,128)(2,1)S(1)} %get-tuple-element.127, f32[10,256,256]{2,1,0:T(8,128)S(1)} %maximum_convert_fusion), kind=kLoop, calls=%fused_computation.128 | loop fusion | flops 5502464 | bytes 5253120 | tf_op jit(solution)/shard_map/reduce_sum | solution.py:58
  81.0 1.8 fusion.20
  83.2 3.5 %concatenate.11 = f32[51,256]{1,0:T(8,128)S(1)} concatenate(f32[1,256]{1,0:T(1,128)} %bitcast.346, f32[1,256]{1,0:T(1,128)S(1)} %bitcast.327, f32[1,256]{1,0:T(1,128)S(1)} %bitcast.328, f32[1,256]{1,0:T(1,128)S(1)} %bitcast.329, f32[1,256]{1,0:T(1,128)S(1)} %bitcast.330, f32[1,256]{1,0:T(1,128)S(1)} %bitcast.331, f32[1,256]{1,0:T(1,128)S(1)} %bitcast.332, ...), dimensions={0} | concatenate | bytes 104448 | tf_op jit(solution)/shard_map/concatenate | solution.py:156
  86.7 62.9 %psum.7 = f32[51,256]{1,0:T(8,128)} all-reduce(f32[51,256]{1,0:T(8,128)S(1)} %concatenate.11), channel_id=1, replica_groups=mesh['group'=2,'row'=16] {'row'}, use_global_device_ids=true, to_apply=%region_59.60 | all-reduce | flops 13056 | bytes 104448 | tf_op jit(solution)/shard_map/psum | solution.py:157
  149.6 1.3 maximum_convert_fusion.1
  150.9 10.1 %fusion.19 = bf16[4,256,256]{2,1,0:T(8,128)(2,1)} fusion(bf16[4,256,256]{2,1,0:T(8,128)(2,1)} %param.17, f32[10,256,256]{2,1,0:T(8,128)S(1)} %maximum_convert_fusion.1, f32[256]{0:T(256)} %bitcast.256, f32[256]{0:T(256)} %bitcast.258, f32[256]{0:T(256)S(1)} %bitcast.202, f32[256]{0:T(256)S(1)} %bitcast.204, f32[256]{0:T(256)S(1)} %bitcast.206, ...), kind=kLoop, calls=%fused_computation.81 | loop fusion | flops 26214400 | bytes 11060224 | tf_op jit(solution)/shard_map/convert_element_type | solution.py:161
  161.0 24.4 %reduce-scatter.3.cloned.1.call-done = f32[16,1024]{1,0:T(8,128)} async-done(((f32[256,1024]{1,0:T(8,128)}), f32[16,1024]{1,0:T(8,128)}) %reduce-scatter.3.cloned.1.call-update) | async-done | bytes 65552 | tf_op jit(solution)/shard_map/reduce_scatter | solution.py:123
  (161 shorter events, 14.3 us)
Async XLA Ops:
  7.2 10.7 %copy-start.2 = (bf16[4,256,256]{2,1,0:T(8,128)(2,1)S(1)}, bf16[4,256,256]{2,1,0:T(8,128)(2,1)}, u32[]{:S(2)}) copy-start(bf16[4,256,256]{2,1,0:T(8,128)(2,1)} %param.10) | copy-start | bytes 1572868
  7.2 9.4 %copy-start.14 = (f32[7,7,256]{2,1,0:T(8,128)S(1)}, f32[7,7,256]{2,1,0:T(8,128)}, u32[]{:S(2)}) copy-start(f32[7,7,256]{2,1,0:T(8,128)} %param.12) | copy-start | bytes 150532
  7.2 153.8 %reduce-scatter.5.cloned.1.call-start = ((), (), s32[]{:S(2)}) async-start(), calls=%async_computation.3 | async-start | bytes 1114112 | tf_op jit(solution)/shard_map/reduce_scatter | solution.py:132
  8.5 9.4 %collective-permute-start = (bf16[3,256,256]{2,1,0:T(8,128)(2,1)S(1)}, bf16[3,256,256]{2,1,0:T(8,128)(2,1)S(1)}, u32[]{:S(2)}, u32[]{:S(2)}) collective-permute-start(bf16[3,256,256]{2,1,0:T(8,128)(2,1)S(1)} %get-tuple-element.138), channel_id=1, source_target_pairs={{0,1},{1,2},{2,3},{3,4},{4,5},{5,6},{6,7},{7,8},{8,9},{9,10},{10,1... | collective-permute-start | bytes 1179656 | tf_op jit(solution)/shard_map/ppermute | solution.py:21
  10.8 7.0 %collective-permute-start.1 = (bf16[3,256,256]{2,1,0:T(8,128)(2,1)S(1)}, bf16[3,256,256]{2,1,0:T(8,128)(2,1)}, u32[]{:S(2)}, u32[]{:S(2)}) collective-permute-start(bf16[3,256,256]{2,1,0:T(8,128)(2,1)S(1)} %get-tuple-element.139), channel_id=1, source_target_pairs={{1,0},{2,1},{3,2},{4,3},{5,4},{6,5},{7,6},{8,7},{9,8},{10,9},{11,1... | collective-permute-start | bytes 1179656 | tf_op jit(solution)/shard_map/ppermute | solution.py:24
  12.9 5.0 %copy-start.54 = (f32[256]{0:T(256)}, f32[256]{0:T(256)S(1)}, u32[]{:S(2)}) copy-start(f32[256]{0:T(256)S(1)} %broadcast_bitcast_fusion) | copy-start | bytes 3076
  19.1 11.9 %copy-start.15 = (f32[256]{0:T(256)S(1)}, f32[256]{0:T(256)}, u32[]{:S(2)}) copy-start(f32[256]{0:T(256)} %param.13) | copy-start | bytes 3076
  29.3 4.1 %copy-start.1 = (bf16[256,1024]{1,0:T(8,128)(2,1)S(1)}, bf16[256,1024]{1,0:T(8,128)(2,1)}, u32[]{:S(2)}) copy-start(bf16[256,1024]{1,0:T(8,128)(2,1)} %param.14) | copy-start | bytes 1572868
  33.4 2.9 %copy-start.9 = (f32[2,512,256]{2,1,0:T(8,128)S(1)}, f32[2,512,256]{2,1,0:T(8,128)}, u32[]{:S(2)}) copy-start(f32[2,512,256]{2,1,0:T(8,128)} %get-tuple-element.264) | copy-start | bytes 3145732 | tf_op jit(solution)/shard_map/while
  33.4 2.9 %copy-start.55 = (bf16[1024,256]{1,0:T(8,128)(2,1)S(1)}, bf16[1024,256]{1,0:T(8,128)(2,1)}, u32[]{:S(2)}) copy-start(bf16[1024,256]{1,0:T(8,128)(2,1)} %get-tuple-element.279) | copy-start | bytes 1572868 | tf_op jit(solution)/shard_map/while
  41.7 2.9 %copy-start.9 = (f32[2,512,256]{2,1,0:T(8,128)S(1)}, f32[2,512,256]{2,1,0:T(8,128)}, u32[]{:S(2)}) copy-start(f32[2,512,256]{2,1,0:T(8,128)} %get-tuple-element.264) | copy-start | bytes 3145732 | tf_op jit(solution)/shard_map/while
  41.7 2.9 %copy-start.55 = (bf16[1024,256]{1,0:T(8,128)(2,1)S(1)}, bf16[1024,256]{1,0:T(8,128)(2,1)}, u32[]{:S(2)}) copy-start(bf16[1024,256]{1,0:T(8,128)(2,1)} %get-tuple-element.279) | copy-start | bytes 1572868 | tf_op jit(solution)/shard_map/while
  50.1 2.9 %copy-start = (f32[4,256,256]{2,1,0:T(8,128)S(1)}, f32[4,256,256]{2,1,0:T(8,128)}, u32[]{:S(2)}) copy-start(f32[4,256,256]{2,1,0:T(8,128)} %get-tuple-element.129) | copy-start | bytes 3145732
  56.1 2.7 %copy-start.13 = (bf16[2,512,256]{2,1,0:T(8,128)(2,1)S(1)}, bf16[2,512,256]{2,1,0:T(8,128)(2,1)}, u32[]{:S(2)}) copy-start(bf16[2,512,256]{2,1,0:T(8,128)(2,1)} %get-tuple-element.289) | copy-start | bytes 1572868
  56.1 2.7 %copy-start.56 = (bf16[2,512,1024]{2,1,0:T(8,128)(2,1)S(1)}, bf16[2,512,1024]{2,1,0:T(8,128)(2,1)}, u32[]{:S(2)}) copy-start(bf16[2,512,1024]{2,1,0:T(8,128)(2,1)} %get-tuple-element.58) | copy-start | bytes 6291460
  60.6 124.8 %reduce-scatter.3.cloned.1.call-start = ((), (), s32[]{:S(2)}) async-start(), calls=%async_computation.2 | async-start | bytes 1114112 | tf_op jit(solution)/shard_map/reduce_scatter | solution.py:123
  60.6 88.9 %collective-permute-start.2 = (bf16[3,256,256]{2,1,0:T(8,128)(2,1)}, bf16[3,256,256]{2,1,0:T(8,128)(2,1)}, u32[]{:S(2)}, u32[]{:S(2)}) collective-permute-start(bf16[3,256,256]{2,1,0:T(8,128)(2,1)} %get-tuple-element.136), channel_id=1, source_target_pairs={{0,1},{1,2},{2,3},{3,4},{4,5},{5,6},{6,7},{7,8},{8,9},{9,10},{10,1... | collective-permute-start | bytes 1179656 | tf_op jit(solution)/shard_map/ppermute | solution.py:21
  68.0 81.6 %collective-permute-start.3 = (bf16[3,256,256]{2,1,0:T(8,128)(2,1)S(1)}, bf16[3,256,256]{2,1,0:T(8,128)(2,1)}, u32[]{:S(2)}, u32[]{:S(2)}) collective-permute-start(bf16[3,256,256]{2,1,0:T(8,128)(2,1)S(1)} %get-tuple-element.137), channel_id=1, source_target_pairs={{1,0},{2,1},{3,2},{4,3},{5,4},{6,5},{7,6},{8,7},{9,8},{10,9},{11,1... | collective-permute-start | bytes 1179656 | tf_op jit(solution)/shard_map/ppermute | solution.py:24
  80.2 2.6 %copy-start.16 = (f32[256]{0:T(256)S(1)}, f32[256]{0:T(256)}, u32[]{:S(2)}) copy-start(f32[256]{0:T(256)} %get-tuple-element.107) | copy-start | bytes 3076
  80.3 2.6 %copy-start.17 = (f32[256]{0:T(256)S(1)}, f32[256]{0:T(256)}, u32[]{:S(2)}) copy-start(f32[256]{0:T(256)} %get-tuple-element.98) | copy-start | bytes 3076
  80.3 2.6 %copy-start.18 = (f32[256]{0:T(256)S(1)}, f32[256]{0:T(256)}, u32[]{:S(2)}) copy-start(f32[256]{0:T(256)} %get-tuple-element.99) | copy-start | bytes 3076
  80.3 2.6 %copy-start.19 = (f32[256]{0:T(256)S(1)}, f32[256]{0:T(256)}, u32[]{:S(2)}) copy-start(f32[256]{0:T(256)} %get-tuple-element.100) | copy-start | bytes 3076
  80.3 2.6 %copy-start.20 = (f32[256]{0:T(256)S(1)}, f32[256]{0:T(256)}, u32[]{:S(2)}) copy-start(f32[256]{0:T(256)} %get-tuple-element.101) | copy-start | bytes 3076
  80.3 2.6 %copy-start.21 = (f32[256]{0:T(256)S(1)}, f32[256]{0:T(256)}, u32[]{:S(2)}) copy-start(f32[256]{0:T(256)} %get-tuple-element.102) | copy-start | bytes 3076
  80.3 2.6 %copy-start.22 = (f32[256]{0:T(256)S(1)}, f32[256]{0:T(256)}, u32[]{:S(2)}) copy-start(f32[256]{0:T(256)} %get-tuple-element.103) | copy-start | bytes 3076
  80.3 2.6 %copy-start.23 = (f32[256]{0:T(256)S(1)}, f32[256]{0:T(256)}, u32[]{:S(2)}) copy-start(f32[256]{0:T(256)} %get-tuple-element.104) | copy-start | bytes 3076
  80.3 2.6 %copy-start.24 = (f32[256]{0:T(256)S(1)}, f32[256]{0:T(256)}, u32[]{:S(2)}) copy-start(f32[256]{0:T(256)} %get-tuple-element.105) | copy-start | bytes 3076
  80.3 2.6 %copy-start.25 = (f32[256]{0:T(256)S(1)}, f32[256]{0:T(256)}, u32[]{:S(2)}) copy-start(f32[256]{0:T(256)} %get-tuple-element.106) | copy-start | bytes 3076
  80.3 2.6 %copy-start.26 = (f32[256]{0:T(256)S(1)}, f32[256]{0:T(256)}, u32[]{:S(2)}) copy-start(f32[256]{0:T(256)} %get-tuple-element.79) | copy-start | bytes 3076
  80.4 2.6 %copy-start.27 = (f32[256]{0:T(256)S(1)}, f32[256]{0:T(256)}, u32[]{:S(2)}) copy-start(f32[256]{0:T(256)} %get-tuple-element.80) | copy-start | bytes 3076
  80.4 2.6 %copy-start.28 = (f32[256]{0:T(256)S(1)}, f32[256]{0:T(256)}, u32[]{:S(2)}) copy-start(f32[256]{0:T(256)} %get-tuple-element.81) | copy-start | bytes 3076
  80.4 2.6 %copy-start.29 = (f32[256]{0:T(256)S(1)}, f32[256]{0:T(256)}, u32[]{:S(2)}) copy-start(f32[256]{0:T(256)} %get-tuple-element.82) | copy-start | bytes 3076
  (39 other events, 82.6 us)
Sparse Core Ops, SparseCore 0:
  60.7 63.5 reduce-scatter.4
  128.9 56.4 reduce-scatter.2
where the time goes:
time: 193 us; the launch traced here: 192 us
  blocking collectives  62.9 us (33%)
  other arithmetic  43 us (22%)
  waiting for transfers between devices  24.4 us (13%)
  local copies, waits for them, and re-layouts  17.9 us (9%)
  matrix products  16.5 us (9%)
  between operations  14.9 us (8%)
  starting transfers between devices  12.6 us (7%)
    psum x1, blocking collectives, shards(): small_grads = lax.psum(packed, 'row')  62.9 us
    reduce_scatter x1, waiting for transfers between devices, shards(): lax.psum_scatter(lax.dot_general(section, pre_flat, (((0,), (0,)), ((), (...  24.4 us
    reduce_sum x6, other arithmetic, kernel_terms(): jnp.sum(padded[row_tap:row_tap + image_rows, col_tap:col_tap + image_cols...  10.9 us
    reduce_sum x1, other arithmetic, shards(): centre = jnp.mean(filtered, axis=-1, keepdims=True)  10.2 us
    convert_element_type x1, other arithmetic, shards(): grad_image = (upstream + conv_back).astype(jnp.bfloat16)  10.1 us
    ppermute x2, starting transfers between devices, padded_2(): lax.ppermute(lax.slice_in_dim(block, block.shape[dim] - width, None, axis...  9.77 us
    dot_general x2, matrix products, tile_work(): pre_act = jnp.dot(normed_blk, w_in, preferred_element_type=jnp.float32)  5.8 us
    while x32, local copies, waits for them, and re-layouts  5.38 us
  transfers between devices with their start and end apart: 6, of which 1 were waited for; matrix products, arithmetic and copies ran while one was open for 17% of the time, Pallas kernels for 0%

commit v1 on v0

v1 whole, which is shorter than its diff:
```python
import functools

import jax
import jax.numpy as jnp
from jax import lax
from jax.experimental import pallas as pl
from jax.experimental.pallas import tpu as pltpu
from jax.sharding import PartitionSpec as P

KERNEL = 7
HALF = KERNEL // 2
TILE_COLS = 128
PAD = 16
WIN = 144
FCHUNK = 256

EPSILON = 1e-06
ROOT_TWO_PI = 0.7978845608028654
CUBIC_TERM = 0.044715

BF = jnp.bfloat16
F32 = jnp.float32


def ones_where(shape, rule):
    rows = lax.broadcasted_iota(jnp.int32, shape, 0)
    cols = lax.broadcasted_iota(jnp.int32, shape, 1)
    return jnp.where(rule(rows, cols), 1.0, 0.0).astype(BF)


def mm(a, b, dims=((1,), (0,))):
    return lax.dot_general(a, b, (dims, ((), ())), preferred_element_type=F32)


def other(me, bit):
    step = 1 << bit
    return me + step - 2 * step * ((me // step) % 2)


class Scatter:
    def __init__(self, me, order, bufs, rbufs, ssem, rsem):
        self.me, self.order = me, order
        self.bufs, self.rbufs, self.ssem, self.rsem = bufs, rbufs, ssem, rsem

    def place(self, chunk):
        n = len(self.order)
        return sum(((chunk >> bit) & 1) << (n - 1 - k) for k, bit in enumerate(self.order))

    def halves(self, k):
        half = self.rbufs[k].shape[0]
        mine = (self.me // (1 << self.order[k])) % 2
        return half, mine

    def copy(self, k):
        half, mine = self.halves(k)
        return pltpu.make_async_remote_copy(
            src_ref=self.bufs[k].at[pl.ds((1 - mine) * half, half)],
            dst_ref=self.rbufs[k],
            send_sem=self.ssem.at[k],
            recv_sem=self.rsem.at[k],
            device_id={"row": other(self.me, self.order[k])},
            device_id_type=pl.DeviceIdType.MESH,
        )

    def start(self, k):
        self.copy(k).start()

    def finish(self, k, out_ref):
        self.copy(k).wait()
        half, mine = self.halves(k)
        if k + 1 < len(self.order):
            def step(c, _):
                self.bufs[k + 1][c] = self.bufs[k][mine * half + c] + self.rbufs[k][c]
                return 0

            lax.fori_loop(0, half, step, 0)
            self.start(k + 1)
        else:
            out_ref[...] = self.bufs[k][mine].astype(F32) + self.rbufs[k][0].astype(F32)


def body(
    n, bits,
    tissue_ref, image_ref, kernel_ref, gain_ref, w_in_ref, w_out_ref, scale_ref, cot_ref,
    out_ref, gimg_ref, gwin_ref, gwout_ref, small_ref,
    *scratch,
):
    (ipad, win, kf, kb, shift_f, place_m, place_c, prods, normed_ref, std_ref, istd_ref, grad_ref,
     gbuf, gup, gdn, gshift, kacc, sums, sums_in, pown, pup, pdn) = scratch[:22]
    in_bufs = scratch[22 : 22 + bits]
    in_rbufs = scratch[22 + bits : 22 + 2 * bits]
    out_bufs = scratch[22 + 2 * bits : 22 + 3 * bits]
    out_rbufs = scratch[22 + 3 * bits : 22 + 4 * bits]
    (hs, hr, gs, gr, in_s, in_r, out_s, out_r, sm_s, sm_r) = scratch[22 + 4 * bits :]

    rows, cols, channels = image_ref.shape
    hidden = w_in_ref.shape[1]
    positions = rows * TILE_COLS
    me = lax.axis_index("row")
    has_up = me > 0
    has_dn = me < n - 1

    def signal(target):
        pl.semaphore_signal(
            pltpu.get_barrier_semaphore(), inc=1, device_id={"row": target},
            device_id_type=pl.DeviceIdType.MESH,
        )

    for bit in range(bits):
        signal(other(me, bit))

    @pl.when(has_up)
    def _():
        signal(me - 1)

    @pl.when(has_dn)
    def _():
        signal(me + 1)

    ipad[:, 0:PAD, :] = jnp.zeros((rows + 2 * HALF, PAD, channels), BF)
    ipad[:, PAD + cols :, :] = jnp.zeros((rows + 2 * HALF, PAD, channels), BF)
    edge_rows = jnp.zeros((HALF, cols, channels), BF)
    edge_grad = jnp.zeros(gup.shape, BF)

    @pl.when(me == 0)
    def _():
        ipad[0:HALF, PAD : PAD + cols, :] = edge_rows
        gup[...] = edge_grad

    @pl.when(me == n - 1)
    def _():
        ipad[HALF + rows :, PAD : PAD + cols, :] = edge_rows
        gdn[...] = edge_grad

    count = bits + jnp.where(me > 0, 1, 0) + jnp.where(me < n - 1, 1, 0)
    pl.semaphore_wait(pltpu.get_barrier_semaphore(), count)

    def remote(src, dst, ssem, rsem, target):
        return pltpu.make_async_remote_copy(
            src_ref=src, dst_ref=dst, send_sem=ssem, recv_sem=rsem,
            device_id={"row": target}, device_id_type=pl.DeviceIdType.MESH,
        )

    def halo_dn():
        return remote(image_ref.at[rows - HALF : rows], ipad.at[0:HALF, PAD : PAD + cols],
                      hs.at[0], hr.at[0], me + 1)

    def halo_up():
        return remote(image_ref.at[0:HALF], ipad.at[HALF + rows : rows + 2 * HALF, PAD : PAD + cols],
                      hs.at[1], hr.at[1], me - 1)

    @pl.when(has_dn)
    def _():
        halo_dn().start()

    @pl.when(has_up)
    def _():
        halo_up().start()

    tile = tissue_ref[0, 1]
    flag = tile.astype(F32)
    in_right = jnp.full((1, 1), flag, F32).astype(BF)
    in_left = jnp.full((1, 1), 1.0 - flag, F32).astype(BF)

    def at_tile(ref, r, width):
        left, right = ref[r, 0:width, :], ref[r, TILE_COLS : TILE_COLS + width, :]
        return left * in_left + right * in_right

    ipad[HALF : HALF + rows, PAD : PAD + cols, :] = image_ref[...]
    for i in range(KERNEL):
        for j in range(KERNEL):
            tap = kernel_ref[i, j : j + 1, :]
            kf[i * KERNEL + j] = jnp.broadcast_to(tap, (8, channels))
            kb[i * KERNEL + j] = jnp.broadcast_to(tap, (16, channels)).astype(BF)
    for j in range(KERNEL):
        shift_f[:, j * WIN : (j + 1) * WIN] = ones_where((TILE_COLS, WIN), lambda w, x: x == w + j)
        lanes = slice(j * TILE_COLS, (j + 1) * TILE_COLS)
        low = ones_where((TILE_COLS, TILE_COLS), lambda b, w: w == b - j + HALF)
        right = ones_where((TILE_COLS, TILE_COLS), lambda b, w: w == b - TILE_COLS - j + HALF)
        left = ones_where((TILE_COLS, TILE_COLS), lambda b, w: w == b + TILE_COLS - j + HALF)
        place_m[0:TILE_COLS, lanes] = low
        place_m[TILE_COLS:, lanes] = left
        place_c[0:TILE_COLS, lanes] = right - low
        place_c[TILE_COLS:, lanes] = low - left
    select = ones_where((WIN, WIN + PAD), lambda x, y: y == x + PAD - HALF)
    scale = scale_ref[...]
    gain = gain_ref[...]
    for a in range(rows):
        span = slice(a * TILE_COLS, (a + 1) * TILE_COLS)
        upstream = at_tile(cot_ref, a, TILE_COLS).astype(F32)
        grad_ref[span, :] = (scale * upstream).astype(BF)

    def window(r):
        win[r] = mm(select, at_tile(ipad, r, WIN + PAD)).astype(BF)

    for r in range(HALF, HALF + rows):
        window(r)

    @pl.when(has_up)
    def _():
        halo_dn().wait_recv()

    for r in range(HALF):
        window(r)

    @pl.when(has_dn)
    def _():
        halo_up().wait_recv()

    for r in range(HALF + rows, rows + 2 * HALF):
        window(r)

    def conv_step(c, _):
        at = pl.ds(pl.multiple_of(c * 16, 16), 16)
        for lanes in (slice(0, 128), slice(128, 256)):
            lines = [win[r, at, lanes].astype(F32) for r in range(rows + 2 * HALF)]
            for j in range(KERNEL):
                taps = [kf[i * KERNEL + j, :, lanes] for i in range(KERNEL)]
                for a in range(rows):
                    total = lines[a] * jnp.concatenate([taps[0]] * 2, axis=0)
                    for i in range(1, KERNEL):
                        total = total + lines[a + i] * jnp.concatenate([taps[i]] * 2, axis=0)
                    prods[a, j, at, lanes] = total.astype(BF)
        return 0

    lax.fori_loop(0, WIN // 16, conv_step, 0)

    for a in range(rows):
        span = slice(a * TILE_COLS, (a + 1) * TILE_COLS)
        filtered = mm(shift_f[...], prods[a].reshape(KERNEL * WIN, channels))
        centred = filtered - jnp.mean(filtered, axis=-1, keepdims=True)
        inv_std = lax.rsqrt(jnp.mean(centred * centred, axis=-1, keepdims=True) + EPSILON)
        standard = centred * inv_std
        std_ref[span, :] = standard
        istd_ref[span, :] = inv_std
        normed_ref[span, :] = (standard * gain).astype(BF)

    scat_in = Scatter(me, [0] + list(range(2, bits)) + [1], in_bufs, in_rbufs, in_s, in_r)
    scat_out = Scatter(me, list(range(bits)), out_bufs, out_rbufs, out_s, out_r)
    in_rows = gwin_ref.shape[0]
    out_rows = gwout_ref.shape[0]

    normed = normed_ref[...]
    grads = grad_ref[...]
    branch = jnp.zeros((positions, channels), F32)
    grad_norm = jnp.zeros((positions, channels), F32)
    for f in range(hidden // FCHUNK):
        fs = slice(f * FCHUNK, (f + 1) * FCHUNK)
        w_in = w_in_ref[:, fs]
        w_out = w_out_ref[fs, :]
        z = mm(normed, w_in)
        zz = z * z
        tangent = jnp.tanh(z * (ROOT_TWO_PI + (ROOT_TWO_PI * CUBIC_TERM) * zz))
        half_up = 0.5 + 0.5 * tangent
        act = (z * half_up).astype(BF)
        slope = half_up + z * (half_up * (1.0 - tangent)) * (
            ROOT_TWO_PI + (3.0 * ROOT_TWO_PI * CUBIC_TERM) * zz
        )
        branch = branch + mm(act, w_out)
        grad_pre = (mm(grads, w_out, ((1,), (1,))) * slope).astype(BF)
        grad_norm = grad_norm + mm(grad_pre, w_in, ((1,), (1,)))
        part = mm(act, grads, ((0,), (0,))).astype(BF)
        per = FCHUNK // out_rows
        for q in range(per):
            out_bufs[0][scat_out.place(f * per + q)] = part[q * out_rows : (q + 1) * out_rows]
        part = mm(normed, grad_pre, ((0,), (0,))).astype(BF)
        for q in range(n):
            in_bufs[0][scat_in.place(q), :, fs] = part[q * in_rows : (q + 1) * in_rows]
    scat_out.start(0)
    scat_in.start(0)

    standard = std_ref[...]
    grad_std = grad_norm * gain
    mean_g = jnp.mean(grad_std, axis=-1, keepdims=True)
    mean_s = jnp.mean(grad_std * standard, axis=-1, keepdims=True)
    grad_conv = (istd_ref[...] * (grad_std - mean_g - standard * mean_s)).astype(BF)
    gbuf[16 : 16 + positions, :] = grad_conv
    flags = jnp.full((16, channels), flag, F32).astype(BF)
    gbuf[0:16, :] = flags
    gbuf[16 + positions :, :] = flags
    reach = HALF * TILE_COLS

    def grad_up():
        return remote(gbuf.at[0 : 16 + reach], gdn, gs.at[0], gr.at[0], me - 1)

    def grad_dn():
        return remote(gbuf.at[16 + positions - reach : 32 + positions], gup, gs.at[1], gr.at[1], me + 1)

    @pl.when(has_up)
    def _():
        grad_up().start()

    @pl.when(has_dn)
    def _():
        grad_dn().start()

    scale_sum = jnp.zeros((1, channels), F32)
    for a in range(rows):
        span = slice(a * TILE_COLS, (a + 1) * TILE_COLS)
        upstream = at_tile(cot_ref, a, TILE_COLS).astype(F32)
        scale_sum = scale_sum + jnp.sum(branch[span] * upstream, axis=0, keepdims=True)
        added = scale * branch[span]
        for s in range(2):
            weight = flag if s == 1 else 1.0 - flag
            cs = slice(s * TILE_COLS, (s + 1) * TILE_COLS)
            out_ref[a, cs, :] = (image_ref[a, cs, :].astype(F32) + weight * added).astype(BF)
    gain_sum = jnp.sum(grad_norm * standard, axis=0, keepdims=True)

    scat_out.finish(0, None)
    scat_in.finish(0, None)

    for h in range(rows):
        line = grad_conv[h * TILE_COLS : (h + 1) * TILE_COLS]
        for j in range(KERNEL):
            gshift[j, h] = mm(
                shift_f[:, j * WIN : (j + 1) * WIN], line, ((0,), (0,))
            ).astype(BF)
    kacc[...] = jnp.zeros(kacc.shape, F32)

    def kernel_step(c, _):
        at = pl.ds(pl.multiple_of(c * 16, 16), 16)
        lines = [win[r, at, :] for r in range(rows + 2 * HALF)]
        for j in range(KERNEL):
            shifted = [gshift[j, h, at, :] for h in range(rows)]
            for i in range(KERNEL):
                total = lines[i] * shifted[0]
                for h in range(1, rows):
                    total = total + lines[i + h] * shifted[h]
                total = total.astype(F32)
                kacc[i * KERNEL + j] += total[0:8] + total[8:16]
        return 0

    lax.fori_loop(0, WIN // 16, kernel_step, 0)
    for t in range(KERNEL * KERNEL):
        sums[0, t : t + 1, :] = jnp.sum(kacc[t], axis=0, keepdims=True)
    sums[0, 49:50, :] = gain_sum
    sums[0, 50:51, :] = scale_sum
    sums[0, 51:, :] = jnp.zeros((sums.shape[1] - 51, channels), F32)

    def small(k):
        return remote(sums.at[k], sums_in.at[k], sm_s.at[k], sm_r.at[k], other(me, k))

    small(0).start()
    scat_out.finish(1, None)
    scat_in.finish(1, None)

    def back_step(c, _):
        at = pl.ds(pl.multiple_of(c * 16, 16), 16)
        own = [gbuf[pl.ds(pl.multiple_of(16 + h * TILE_COLS + c * 16, 16), 16), :] for h in range(rows)]
        for j in range(KERNEL):
            taps = [kb[i * KERNEL + j] for i in range(KERNEL)]
            for a in range(rows):
                total = own[0] * taps[a + HALF]
                for r in range(1, rows):
                    total = total + own[r] * taps[a - r + HALF]
                pown[a, j, at, :] = total
        return 0

    lax.fori_loop(0, TILE_COLS // 16, back_step, 0)

    def small_next(k):
        small(k).wait()
        if k + 1 < bits:
            sums[k + 1] = sums[k] + sums_in[k]
            small(k + 1).start()
        else:
            small_ref[...] = (sums[k] + sums_in[k])[: small_ref.shape[0]]

    small_next(0)

    @pl.when(has_up)
    def _():
        grad_dn().wait_recv()

    @pl.when(has_dn)
    def _():
        grad_up().wait_recv()

    def halo_step(c, _):
        at = pl.ds(pl.multiple_of(c * 16, 16), 16)
        above = [gup[pl.ds(pl.multiple_of(u * TILE_COLS + c * 16, 16), 16), :] for u in range(HALF)]
        below = [gdn[pl.ds(pl.multiple_of(16 + u * TILE_COLS + c * 16, 16), 16), :] for u in range(HALF)]
        for j in range(KERNEL):
            taps = [kb[i * KERNEL + j] for i in range(KERNEL)]
            for a in range(HALF):
                total = above[a] * taps[KERNEL - 1]
                for u in range(a + 1, HALF):
                    total = total + above[u] * taps[a - u + KERNEL - 1]
                pup[a, j, at, :] = total
            for a in range(rows - HALF, rows):
                total = below[0] * taps[a + HALF - rows]
                for v in range(1, a + HALF - rows + 1):
                    total = total + below[v] * taps[a + HALF - rows - v]
                pdn[a - (rows - HALF), j, at, :] = total
        return 0

    lax.fori_loop(0, TILE_COLS // 16, halo_step, 0)

    def placing(value):
        return place_m[...] + place_c[...] * value

    depth = KERNEL * TILE_COLS
    at_own = placing(in_right)
    at_up = placing(gup[reach : reach + 1, 0:1])
    at_dn = placing(gdn[0:1, 0:1])
    for a in range(rows):
        total = mm(at_own, pown[a].reshape(depth, channels))
        if a < HALF:
            total = total + mm(at_up, pup[a].reshape(depth, channels))
        if a >= rows - HALF:
            total = total + mm(at_dn, pdn[a - (rows - HALF)].reshape(depth, channels))
        gimg_ref[a] = (cot_ref[a].astype(F32) + total).astype(BF)

    for k in range(2, bits):
        scat_out.finish(k, gwout_ref)
        scat_in.finish(k, gwin_ref)
        small_next(k - 1)
    small_next(bits - 1)

    @pl.when(has_dn)
    def _():
        halo_dn().wait_send()
        grad_dn().wait_send()

    @pl.when(has_up)
    def _():
        halo_up().wait_send()
        grad_up().wait_send()


def shards(n, image, tissue, kernel, ln_gain, w_in, w_out, layer_scale, cotangent):
    rows, cols, channels = image.shape
    hidden = w_in.shape[1]
    bits = n.bit_length() - 1
    in_rows, out_rows = channels // n, hidden // n
    positions = rows * TILE_COLS
    halo = HALF * TILE_COLS + 16
    vmem = pltpu.VMEM
    scratch = [
        vmem((rows + 2 * HALF, cols + 2 * PAD, channels), BF),
        vmem((rows + 2 * HALF, WIN, channels), BF),
        vmem((KERNEL * KERNEL, 8, channels), F32),
        vmem((KERNEL * KERNEL, 16, channels), BF),
        vmem((TILE_COLS, KERNEL * WIN), BF),
        vmem((2 * TILE_COLS, KERNEL * TILE_COLS), BF),
        vmem((2 * TILE_COLS, KERNEL * TILE_COLS), BF),
        vmem((rows, KERNEL, WIN, channels), BF),
        vmem((positions, channels), BF),
        vmem((positions, channels), F32),
        vmem((positions, 1), F32),
        vmem((positions, channels), BF),
        vmem((positions + 32, channels), BF),
        vmem((halo, channels), BF),
        vmem((halo, channels), BF),
        vmem((KERNEL, rows, WIN, channels), BF),
        vmem((KERNEL * KERNEL, 8, channels), F32),
        vmem((bits, 56, channels), F32),
        vmem((bits, 56, channels), F32),
        vmem((rows, KERNEL, TILE_COLS, channels), BF),
        vmem((HALF, KERNEL, TILE_COLS, channels), BF),
        vmem((HALF, KERNEL, TILE_COLS, channels), BF),
    ]
    for shape in ((in_rows, hidden), (out_rows, channels)):
        scratch += [vmem((n >> k,) + shape, BF) for k in range(bits)]
        scratch += [vmem((n >> (k + 1),) + shape, BF) for k in range(bits)]
    dma = pltpu.SemaphoreType.DMA
    scratch += [dma((2,))] * 4 + [dma((bits,))] * 6
    whole = pl.BlockSpec(memory_space=pltpu.VMEM)
    return pl.pallas_call(
        functools.partial(body, n, bits),
        out_shape=(
            jax.ShapeDtypeStruct((rows, cols, channels), BF),
            jax.ShapeDtypeStruct((rows, cols, channels), BF),
            jax.ShapeDtypeStruct((in_rows, hidden), F32),
            jax.ShapeDtypeStruct((out_rows, channels), F32),
            jax.ShapeDtypeStruct((KERNEL * KERNEL + 2, channels), F32),
        ),
        in_specs=[pl.BlockSpec(memory_space=pltpu.SMEM)] + [whole] * 7,
        out_specs=(whole,) * 5,
        scratch_shapes=scratch,
        compiler_params=pltpu.CompilerParams(
            collective_id=0, has_side_effects=True, vmem_limit_bytes=48 * 1024 * 1024
        ),
    )(
        tissue, image, kernel, ln_gain.reshape(1, channels), w_in, w_out,
        layer_scale.reshape(1, channels), cotangent,
    )


def solution(mesh):
    placed = (
        P(("group", "row"), None, None),
        P(("group", "row"), None),
        P(),
        P(),
        P(),
        P(),
        P(),
        P(("group", "row"), None, None),
    )
    return jax.shard_map(
        functools.partial(shards, mesh.shape["row"]),
        mesh=mesh,
        in_specs=placed,
        out_specs=(
            P(("group", "row"), None, None),
            P(("group", "row"), None, None),
            P(("group", "row"), None),
            P(("group", "row"), None),
            P("group", None),
        ),
        check_vma=False,
    )
```

time: 193 us -> 50.9 us (0.26)
  blocking collectives: 62.9 us -> 0 us
  other arithmetic: 43 us -> 0 us
  Pallas kernels: 0 us -> 40.7 us
  waiting for transfers between devices: 24.4 us -> 0 us
  matrix products: 16.5 us -> 0 us
  between operations: 14.9 us -> 0.67 us
  starting transfers between devices: 12.6 us -> 0 us
  local copies, waits for them, and re-layouts: 17.9 us -> 9.13 us
    psum x1 -> x0, blocking collectives: 62.9 us -> none  [shards(): small_grads = lax.psum(packed, 'row')]
    pallas_call x0 -> x1, Pallas kernels: none -> 40.7 us  [shards(): pl.pallas_call(functools.partial(body, n, bits), out_shape=(jax.ShapeDtyp...]
    reduce_sum x11 -> x0, other arithmetic: 26.9 us -> none  [the longest x6 10.9 us: kernel_terms(): jnp.sum(padded[row_tap:row_tap + image_rows, col_tap:col_tap + image_cols...]
    reduce_scatter x2 -> x0, waiting for transfers between devices: 24.4 us -> none  [the longest x1 24.4 us: shards(): lax.psum_scatter(lax.dot_general(section, pre_flat, (((0,), (0,)), ((), (...]
    dot_general x10 -> x0, matrix products: 16.5 us -> none  [the longest x2 5.8 us: tile_work(): pre_act = jnp.dot(normed_blk, w_in, preferred_element_type=jnp.float32)]
    convert_element_type x6 -> x0, other arithmetic: 16 us -> none  [the longest x1 10.1 us: shards(): grad_image = (upstream + conv_back).astype(jnp.bfloat16)]
    ppermute x4 -> x0, starting transfers between devices: 12.5 us -> none  [the longest x2 9.77 us: padded_2(): lax.ppermute(lax.slice_in_dim(block, block.shape[dim] - width, None, axis...]
    unnamed x99 -> x21, local copies, waits for them, and re-layouts: 1.02 us -> 9.13 us
  transfers between devices with their start and end apart: 6 -> 0, of which waited for: 1 -> 0; matrix products, arithmetic and copies ran while one was open for 17% -> 0% of each run, Pallas kernels for 0% -> 0%
where the time goes in v1:
time: 50.9 us; the launch traced here: 50.5 us
  Pallas kernels  40.7 us (80%)
  local copies, waits for them, and re-layouts  9.13 us (18%)
  between operations  0.67 us (1%)
    pallas_call x1, Pallas kernels, shards(): pl.pallas_call(functools.partial(body, n, bits), out_shape=(jax.ShapeDtyp...  40.7 us
    unnamed x21, local copies, waits for them, and re-layouts  9.13 us

profile of v1, /device:TPU:0, one launch (start us, length us, event | category | flops | bytes accessed | tf_op | source)
XLA Modules:
  0.0 50.5 jit_solution(4431693327682389696)
XLA Ops:
  0.6 0.0 copy-start.6
  0.6 0.0 copy-start.5
  0.7 0.0 copy-start.7
  0.7 0.7 %copy-done.6 = f32[256]{0:T(256)S(1)} copy-done((f32[256]{0:T(256)S(1)}, f32[256]{0:T(256)}, u32[]{:S(2)}) %copy-start.6) | copy-done | bytes 1048
  1.3 0.0 copy-done.5
  1.3 0.0 copy-done.7
  1.3 0.0 copy-start
  1.3 1.0 %copy-done = bf16[4,256,256]{2,1,0:T(8,128)(2,1)S(1)} copy-done((bf16[4,256,256]{2,1,0:T(8,128)(2,1)S(1)}, bf16[4,256,256]{2,1,0:T(8,128)(2,1)}, u32[]{:S(2)}) %copy-start) | copy-done | bytes 524312
  2.4 0.0 copy-start.1
  2.4 1.0 %copy-done.1 = bf16[256,1024]{1,0:T(8,128)(2,1)S(1)} copy-done((bf16[256,1024]{1,0:T(8,128)(2,1)S(1)}, bf16[256,1024]{1,0:T(8,128)(2,1)}, u32[]{:S(2)}) %copy-start.1) | copy-done | bytes 524312
  3.4 0.0 copy-start.2
  3.4 1.0 %copy-done.2 = bf16[1024,256]{1,0:T(8,128)(2,1)S(1)} copy-done((bf16[1024,256]{1,0:T(8,128)(2,1)S(1)}, bf16[1024,256]{1,0:T(8,128)(2,1)}, u32[]{:S(2)}) %copy-start.2) | copy-done | bytes 524312
  4.5 0.0 copy-start.3
  4.5 1.0 %copy-done.3 = bf16[4,256,256]{2,1,0:T(8,128)(2,1)S(1)} copy-done((bf16[4,256,256]{2,1,0:T(8,128)(2,1)S(1)}, bf16[4,256,256]{2,1,0:T(8,128)(2,1)}, u32[]{:S(2)}) %copy-start.3) | copy-done | bytes 524312
  5.5 0.0 copy-start.4
  5.5 0.8 %copy-done.4 = f32[7,7,256]{2,1,0:T(8,128)S(1)} copy-done((f32[7,7,256]{2,1,0:T(8,128)S(1)}, f32[7,7,256]{2,1,0:T(8,128)}, u32[]{:S(2)}) %copy-start.4) | copy-done | bytes 50200
  6.3 40.7 %shard_map.119 = (bf16[4,256,256]{2,1,0:T(8,128)(2,1)S(1)}, bf16[4,256,256]{2,1,0:T(8,128)(2,1)S(1)}, f32[16,1024]{1,0:T(8,128)S(1)}, f32[64,256]{1,0:T(8,128)S(1)}, f32[51,256]{1,0:T(8,128)S(1)}) custom-call(s32[1,2]{1,0:T(1,128)S(1)} %copy-done.7, bf16[4,256,256]{2,1,0:T(8,128)(2,1)S(1)} %copy-done, f32[7,7,256]{2,1,0:T(8,128)S(1)} %copy-done.4, ...), custom_call_target="tpu_custom_call" | custom-call | tf_op jit(solution)/shard_map/pallas_call | solution.py:469
  47.0 0.8 %copy.18 = bf16[4,256,256]{2,1,0:T(8,128)(2,1)} copy(bf16[4,256,256]{2,1,0:T(8,128)(2,1)S(1)} %get-tuple-element.10) | data formatting | bytes 1048576
  47.8 0.8 %copy.19 = bf16[4,256,256]{2,1,0:T(8,128)(2,1)} copy(bf16[4,256,256]{2,1,0:T(8,128)(2,1)S(1)} %get-tuple-element.11) | data formatting | bytes 1048576
  48.6 0.6 %copy.20 = f32[16,1024]{1,0:T(8,128)} copy(f32[16,1024]{1,0:T(8,128)S(1)} %get-tuple-element.12) | data formatting | bytes 131072
  49.3 0.6 %copy.21 = f32[64,256]{1,0:T(8,128)} copy(f32[64,256]{1,0:T(8,128)S(1)} %get-tuple-element.13) | data formatting | bytes 131072
  49.9 0.6 %copy.22 = f32[51,256]{1,0:T(8,128)} copy(f32[51,256]{1,0:T(8,128)S(1)} %get-tuple-element.14) | data formatting | bytes 104448
Async XLA Ops:
  0.6 0.7 %copy-start.6 = (f32[256]{0:T(256)S(1)}, f32[256]{0:T(256)}, u32[]{:S(2)}) copy-start(f32[256]{0:T(256)} %param.14) | copy-start | bytes 3076
  0.6 0.7 %copy-start.5 = (f32[256]{0:T(256)S(1)}, f32[256]{0:T(256)}, u32[]{:S(2)}) copy-start(f32[256]{0:T(256)} %param.11) | copy-start | bytes 3076
  0.7 0.7 %copy-start.7 = (s32[1,2]{1,0:T(1,128)S(1)}, s32[1,2]{1,0:T(1,128)}, u32[]{:S(2)}) copy-start(s32[1,2]{1,0:T(1,128)} %tissue_ref.1) | copy-start | bytes 28
  1.3 1.0 %copy-start = (bf16[4,256,256]{2,1,0:T(8,128)(2,1)S(1)}, bf16[4,256,256]{2,1,0:T(8,128)(2,1)}, u32[]{:S(2)}) copy-start(bf16[4,256,256]{2,1,0:T(8,128)(2,1)} %image_ref.1) | copy-start | bytes 1572868
  2.4 1.0 %copy-start.1 = (bf16[256,1024]{1,0:T(8,128)(2,1)S(1)}, bf16[256,1024]{1,0:T(8,128)(2,1)}, u32[]{:S(2)}) copy-start(bf16[256,1024]{1,0:T(8,128)(2,1)} %w_in_ref.1) | copy-start | bytes 1572868
  3.4 1.0 %copy-start.2 = (bf16[1024,256]{1,0:T(8,128)(2,1)S(1)}, bf16[1024,256]{1,0:T(8,128)(2,1)}, u32[]{:S(2)}) copy-start(bf16[1024,256]{1,0:T(8,128)(2,1)} %w_out_ref.1) | copy-start | bytes 1572868
  4.5 1.0 %copy-start.3 = (bf16[4,256,256]{2,1,0:T(8,128)(2,1)S(1)}, bf16[4,256,256]{2,1,0:T(8,128)(2,1)}, u32[]{:S(2)}) copy-start(bf16[4,256,256]{2,1,0:T(8,128)(2,1)} %cot_ref.1) | copy-start | bytes 1572868
  5.5 0.8 %copy-start.4 = (f32[7,7,256]{2,1,0:T(8,128)S(1)}, f32[7,7,256]{2,1,0:T(8,128)}, u32[]{:S(2)}) copy-start(f32[7,7,256]{2,1,0:T(8,128)} %kernel_ref.1) | copy-start | bytes 150532

commit v2 on v1

--- a/solution.py
+++ b/solution.py
@@ -81,8 +81,8 @@
 
 def body(
     n, bits,
-    tissue_ref, image_ref, kernel_ref, gain_ref, w_in_ref, w_out_ref, scale_ref, cot_ref,
-    out_ref, gimg_ref, gwin_ref, gwout_ref, small_ref,
+    tissue_ref, image_ref, kernel_hbm, gain_hbm, w_in_hbm, w_out_hbm, scale_hbm, cot_hbm,
+    out_hbm, gimg_hbm, gwin_hbm, gwout_hbm, small_hbm,
     *scratch,
 ):
     (ipad, win, kf, kb, shift_f, place_m, place_c, prods, normed_ref, std_ref, istd_ref, grad_ref,
@@ -91,12 +91,31 @@
     in_rbufs = scratch[22 + bits : 22 + 2 * bits]
     out_bufs = scratch[22 + 2 * bits : 22 + 3 * bits]
     out_rbufs = scratch[22 + 3 * bits : 22 + 4 * bits]
-    (hs, hr, gs, gr, in_s, in_r, out_s, out_r, sm_s, sm_r) = scratch[22 + 4 * bits :]
-
+    (hs, hr, gs, gr, in_s, in_r, out_s, out_r, sm_s, sm_r) = scratch[22 + 4 * bits : 22 + 4 * bits + 10]
+
+    kernel_ref, gain_ref, w_in_ref, w_out_ref, scale_ref, cot_ref, load_sem = scratch[22 + 4 * bits + 10 : -6]
+    out_ref, gimg_ref, gwin_ref, gwout_ref, small_ref, store_sem = scratch[-6:]
+    stores = [
+        pltpu.make_async_copy(src, dst, store_sem.at[k])
+        for k, (src, dst) in enumerate((
+            (out_ref, out_hbm), (gimg_ref, gimg_hbm), (gwin_ref, gwin_hbm),
+            (gwout_ref, gwout_hbm), (small_ref, small_hbm),
+        ))
+    ]
     rows, cols, channels = image_ref.shape
     hidden = w_in_ref.shape[1]
     positions = rows * TILE_COLS
     me = lax.axis_index("row")
+    loads = [
+        pltpu.make_async_copy(src, dst, load_sem.at[k])
+        for k, (src, dst) in enumerate((
+            (image_ref, ipad.at[HALF : HALF + rows, PAD : PAD + cols]),
+            (kernel_hbm, kernel_ref), (gain_hbm, gain_ref), (scale_hbm, scale_ref),
+            (cot_hbm, cot_ref), (w_in_hbm, w_in_ref), (w_out_hbm, w_out_ref),
+        ))
+    ]
+    for load in loads:
+        load.start()
     has_up = me > 0
     has_dn = me < n - 1
 
@@ -166,7 +185,7 @@
         left, right = ref[r, 0:width, :], ref[r, TILE_COLS : TILE_COLS + width, :]
         return left * in_left + right * in_right
 
-    ipad[HALF : HALF + rows, PAD : PAD + cols, :] = image_ref[...]
+    loads[1].wait()
     for i in range(KERNEL):
         for j in range(KERNEL):
             tap = kernel_ref[i, j : j + 1, :]
@@ -183,6 +202,8 @@
         place_c[0:TILE_COLS, lanes] = right - low
         place_c[TILE_COLS:, lanes] = low - left
     select = ones_where((WIN, WIN + PAD), lambda x, y: y == x + PAD - HALF)
+    for load in loads[2:5]:
+        load.wait()
     scale = scale_ref[...]
     gain = gain_ref[...]
     for a in range(rows):
@@ -193,6 +214,7 @@
     def window(r):
         win[r] = mm(select, at_tile(ipad, r, WIN + PAD)).astype(BF)
 
+    loads[0].wait()
     for r in range(HALF, HALF + rows):
         window(r)
 
@@ -240,6 +262,8 @@
     in_rows = gwin_ref.shape[0]
     out_rows = gwout_ref.shape[0]
 
+    loads[5].wait()
+    loads[6].wait()
     normed = normed_ref[...]
     grads = grad_ref[...]
     branch = jnp.zeros((positions, channels), F32)
@@ -303,7 +327,8 @@
         for s in range(2):
             weight = flag if s == 1 else 1.0 - flag
             cs = slice(s * TILE_COLS, (s + 1) * TILE_COLS)
-            out_ref[a, cs, :] = (image_ref[a, cs, :].astype(F32) + weight * added).astype(BF)
+            out_ref[a, cs, :] = (ipad[HALF + a, PAD + cs.start : PAD + cs.stop, :].astype(F32) + weight * added).astype(BF)
+    stores[0].start()
     gain_sum = jnp.sum(grad_norm * standard, axis=0, keepdims=True)
 
     scat_out.finish(0, None)
@@ -367,6 +392,8 @@
             small_ref[...] = (sums[k] + sums_in[k])[: small_ref.shape[0]]
 
     small_next(0)
+    scat_out.finish(2, gwout_ref)
+    scat_in.finish(2, gwin_ref)
 
     @pl.when(has_up)
     def _():
@@ -395,6 +422,7 @@
         return 0
 
     lax.fori_loop(0, TILE_COLS // 16, halo_step, 0)
+    small_next(1)
 
     def placing(value):
         return place_m[...] + place_c[...] * value
@@ -410,12 +438,16 @@
         if a >= rows - HALF:
             total = total + mm(at_dn, pdn[a - (rows - HALF)].reshape(depth, channels))
         gimg_ref[a] = (cot_ref[a].astype(F32) + total).astype(BF)
-
-    for k in range(2, bits):
+        if a == 1:
+            small_next(2)
+
+    stores[1].start()
+    for k in range(3, bits):
         scat_out.finish(k, gwout_ref)
         scat_in.finish(k, gwin_ref)
-        small_next(k - 1)
-    small_next(bits - 1)
+        small_next(k)
+    for store in stores[2:]:
+        store.start()
 
     @pl.when(has_dn)
     def _():
@@ -426,6 +458,18 @@
     def _():
         halo_up().wait_send()
         grad_up().wait_send()
+
+    for store in stores:
+        store.wait()
+
+
+def copy_out(*refs):
+    sem = refs[-1]
+    copies = [pltpu.make_async_copy(refs[k], refs[5 + k], sem.at[k]) for k in range(5)]
+    for copy in copies:
+        copy.start()
+    for copy in copies:
+        copy.wait()
 
 
 def shards(n, image, tissue, kernel, ln_gain, w_in, w_out, layer_scale, cotangent):
@@ -436,6 +480,13 @@
     positions = rows * TILE_COLS
     halo = HALF * TILE_COLS + 16
     vmem = pltpu.VMEM
+    outputs = (
+        jax.ShapeDtypeStruct((rows, cols, channels), BF),
+        jax.ShapeDtypeStruct((rows, cols, channels), BF),
+        jax.ShapeDtypeStruct((in_rows, hidden), F32),
+        jax.ShapeDtypeStruct((out_rows, channels), F32),
+        jax.ShapeDtypeStruct((KERNEL * KERNEL + 2, channels), F32),
+    )
     scratch = [
         vmem((rows + 2 * HALF, cols + 2 * PAD, channels), BF),
         vmem((rows + 2 * HALF, WIN, channels), BF),
@@ -465,26 +516,31 @@
         scratch += [vmem((n >> (k + 1),) + shape, BF) for k in range(bits)]
     dma = pltpu.SemaphoreType.DMA
     scratch += [dma((2,))] * 4 + [dma((bits,))] * 6
-    whole = pl.BlockSpec(memory_space=pltpu.VMEM)
-    return pl.pallas_call(
+    scratch += [vmem(kernel.shape, F32), vmem((1, channels), F32), vmem(w_in.shape, BF),
+                vmem(w_out.shape, BF), vmem((1, channels), F32), vmem(cotangent.shape, BF), dma((7,))]
+    scratch += [vmem(r.shape, r.dtype) for r in outputs] + [dma((5,))]
+    anywhere = pl.BlockSpec(memory_space=pl.ANY)
+    results = pl.pallas_call(
         functools.partial(body, n, bits),
-        out_shape=(
-            jax.ShapeDtypeStruct((rows, cols, channels), BF),
-            jax.ShapeDtypeStruct((rows, cols, channels), BF),
-            jax.ShapeDtypeStruct((in_rows, hidden), F32),
-            jax.ShapeDtypeStruct((out_rows, channels), F32),
-            jax.ShapeDtypeStruct((KERNEL * KERNEL + 2, channels), F32),
-        ),
-        in_specs=[pl.BlockSpec(memory_space=pltpu.SMEM)] + [whole] * 7,
-        out_specs=(whole,) * 5,
+        out_shape=outputs,
+        in_specs=[pl.BlockSpec(memory_space=pltpu.SMEM)] + [anywhere] * 7,
+        out_specs=(anywhere,) * 5,
         scratch_shapes=scratch,
         compiler_params=pltpu.CompilerParams(
-            collective_id=0, has_side_effects=True, vmem_limit_bytes=48 * 1024 * 1024
+            collective_id=0, has_side_effects=True, vmem_limit_bytes=60 * 1024 * 1024
         ),
     )(
         tissue, image, kernel, ln_gain.reshape(1, channels), w_in, w_out,
         layer_scale.reshape(1, channels), cotangent,
     )
+    return pl.pallas_call(
+        copy_out,
+        out_shape=[jax.ShapeDtypeStruct(r.shape, r.dtype) for r in results],
+        in_specs=[anywhere] * 5,
+        out_specs=[anywhere] * 5,
+        scratch_shapes=[dma((5,))],
+        compiler_params=pltpu.CompilerParams(vmem_limit_bytes=60 * 1024 * 1024),
+    )(*results)
 
 
 def solution(mesh):

time: 50.9 us -> 81.4 us (1.60)
  Pallas kernels: 40.7 us -> 80.6 us
  local copies, waits for them, and re-layouts: 9.13 us -> 0 us
    pallas_call x1 -> x2, Pallas kernels: 40.7 us -> 80.6 us  [the longest x1 42 us: shards(): pl.pallas_call(functools.partial(body, n, bits), out_shape=outputs, in_sp...]
    unnamed x21 -> x0, local copies, waits for them, and re-layouts: 9.13 us -> none
where the time goes in v2:
time: 81.4 us; the launch traced here: 81.3 us
  Pallas kernels  80.6 us (99%)
    pallas_call x1, Pallas kernels, shards(): pl.pallas_call(functools.partial(body, n, bits), out_shape=outputs, in_sp...  42 us
    pallas_call x1, Pallas kernels, shards(): pl.pallas_call(copy_out, out_shape=[jax.ShapeDtypeStruct(r.shape, r.dtype...  38.6 us

profile of v2, /device:TPU:0, one launch (start us, length us, event | category | flops | bytes accessed | tf_op | source)
XLA Modules:
  0.0 81.3 jit_solution(7191283410931449152)
XLA Ops:
  0.6 42.0 %shard_map.119 = (bf16[4,256,256]{2,1,0:T(8,128)(2,1)}, bf16[4,256,256]{2,1,0:T(8,128)(2,1)}, f32[16,1024]{1,0:T(8,128)}, f32[64,256]{1,0:T(8,128)}, f32[51,256]{1,0:T(8,128)}) custom-call(s32[1,2]{1,0:T(1,128)} %tissue_ref.1, bf16[4,256,256]{2,1,0:T(8,128)(2,1)} %image_ref.1, f32[7,7,256]{2,1,0:T(8,128)} %kernel_hbm.1, f32[1,256]{1,0:T(1,128)} %bitcast.2, ...), custom_call_target="tpu_custom_call" | custom-call | tf_op jit(solution)/shard_map/pallas_call | solution.py:523
  42.7 38.6 %shard_map.120 = (bf16[4,256,256]{2,1,0:T(8,128)(2,1)}, bf16[4,256,256]{2,1,0:T(8,128)(2,1)}, f32[16,1024]{1,0:T(8,128)}, f32[64,256]{1,0:T(8,128)}, f32[51,256]{1,0:T(8,128)}) custom-call(bf16[4,256,256]{2,1,0:T(8,128)(2,1)} %get-tuple-element.10.refs_0_, bf16[4,256,256]{2,1,0:T(8,128)(2,1)} %get-tuple-element.11.refs_1_, ...), custom_call_target="tpu_custom_call" | custom-call | tf_op jit(solution)/shard_map/pallas_call | solution.py:536

commit v3 on v2

--- a/solution.py
+++ b/solution.py
@@ -43,8 +43,11 @@
         self.bufs, self.rbufs, self.ssem, self.rsem = bufs, rbufs, ssem, rsem
 
     def place(self, chunk):
+        return (chunk % 2) * self.rbufs[0].shape[0] + chunk // 2
+
+    def place_next(self, chunk):
         n = len(self.order)
-        return sum(((chunk >> bit) & 1) << (n - 1 - k) for k, bit in enumerate(self.order))
+        return sum(((chunk >> bit) & 1) << (n - 1 - k) for k, bit in enumerate(self.order) if k)
 
     def halves(self, k):
         half = self.rbufs[k].shape[0]
@@ -64,6 +67,26 @@
 
     def start(self, k):
         self.copy(k).start()
+
+    def part(self, index, sems, picks):
+        half, mine = self.halves(0)
+        first, *rest = picks
+        return pltpu.make_async_remote_copy(
+            src_ref=self.bufs[0].at[(pl.ds((1 - mine) * half + first.start, first.size), *rest)],
+            dst_ref=self.rbufs[0].at[(first, *rest)],
+            send_sem=sems[0].at[index],
+            recv_sem=sems[1].at[index],
+            device_id={"row": other(self.me, self.order[0])},
+            device_id_type=pl.DeviceIdType.MESH,
+        )
+
+    def finish_parts(self, parts):
+        for part in parts:
+            part.wait()
+        half, mine = self.halves(0)
+        for e in range(half):
+            self.bufs[1][self.place_next(2 * e)] = self.bufs[0][mine * half + e] + self.rbufs[0][e]
+        self.start(1)
 
     def finish(self, k, out_ref):
         self.copy(k).wait()
@@ -93,8 +116,9 @@
     out_rbufs = scratch[22 + 3 * bits : 22 + 4 * bits]
     (hs, hr, gs, gr, in_s, in_r, out_s, out_r, sm_s, sm_r) = scratch[22 + 4 * bits : 22 + 4 * bits + 10]
 
-    kernel_ref, gain_ref, w_in_ref, w_out_ref, scale_ref, cot_ref, load_sem = scratch[22 + 4 * bits + 10 : -6]
+    kernel_ref, gain_ref, w_in_ref, w_out_ref, scale_ref, cot_ref, load_sem = scratch[22 + 4 * bits + 10 : -12]
     out_ref, gimg_ref, gwin_ref, gwout_ref, small_ref, store_sem = scratch[-6:]
+    in0_s, in0_r, out0_s, out0_r, shift_b, conv_part = scratch[-12:-6]
     stores = [
         pltpu.make_async_copy(src, dst, store_sem.at[k])
         for k, (src, dst) in enumerate((
@@ -193,6 +217,7 @@
             kb[i * KERNEL + j] = jnp.broadcast_to(tap, (16, channels)).astype(BF)
     for j in range(KERNEL):
         shift_f[:, j * WIN : (j + 1) * WIN] = ones_where((TILE_COLS, WIN), lambda w, x: x == w + j)
+        shift_b[j] = ones_where((WIN, TILE_COLS), lambda x, w: x == w + j)
         lanes = slice(j * TILE_COLS, (j + 1) * TILE_COLS)
         low = ones_where((TILE_COLS, TILE_COLS), lambda b, w: w == b - j + HALF)
         right = ones_where((TILE_COLS, TILE_COLS), lambda b, w: w == b - TILE_COLS - j + HALF)
@@ -218,6 +243,27 @@
     for r in range(HALF, HALF + rows):
         window(r)
 
+    LANES = (slice(0, 128), slice(128, 256))
+
+    def tap(i, j, lanes):
+        one = kf[i * KERNEL + j, :, lanes]
+        return jnp.concatenate([one, one], axis=0)
+
+    def conv_own(c, _):
+        at = pl.ds(pl.multiple_of(c * 16, 16), 16)
+        for lanes in LANES:
+            lines = [win[HALF + r, at, lanes].astype(F32) for r in range(rows)]
+            for j in range(KERNEL):
+                taps = [tap(i, j, lanes) for i in range(KERNEL)]
+                for a in range(rows):
+                    total = lines[0] * taps[HALF - a]
+                    for r in range(1, rows):
+                        total = total + lines[r] * taps[HALF + r - a]
+                    conv_part[a, j, at, lanes] = total
+        return 0
+
+    lax.fori_loop(0, WIN // 16, conv_own, 0)
+
     @pl.when(has_up)
     def _():
         halo_dn().wait_recv()
@@ -232,20 +278,24 @@
     for r in range(HALF + rows, rows + 2 * HALF):
         window(r)
 
-    def conv_step(c, _):
+    def conv_halo(c, _):
         at = pl.ds(pl.multiple_of(c * 16, 16), 16)
-        for lanes in (slice(0, 128), slice(128, 256)):
-            lines = [win[r, at, lanes].astype(F32) for r in range(rows + 2 * HALF)]
+        for lanes in LANES:
+            lines = {
+                r: win[r, at, lanes].astype(F32)
+                for r in range(rows + 2 * HALF) if not HALF <= r < HALF + rows
+            }
             for j in range(KERNEL):
-                taps = [kf[i * KERNEL + j, :, lanes] for i in range(KERNEL)]
+                taps = [tap(i, j, lanes) for i in range(KERNEL)]
                 for a in range(rows):
-                    total = lines[a] * jnp.concatenate([taps[0]] * 2, axis=0)
-                    for i in range(1, KERNEL):
-                        total = total + lines[a + i] * jnp.concatenate([taps[i]] * 2, axis=0)
+                    total = conv_part[a, j, at, lanes]
+                    for r in lines:
+                        if 0 <= r - a < KERNEL:
+                            total = total + lines[r] * taps[r - a]
                     prods[a, j, at, lanes] = total.astype(BF)
         return 0
 
-    lax.fori_loop(0, WIN // 16, conv_step, 0)
+    lax.fori_loop(0, WIN // 16, conv_halo, 0)
 
     for a in range(rows):
         span = slice(a * TILE_COLS, (a + 1) * TILE_COLS)
@@ -268,6 +318,8 @@
     grads = grad_ref[...]
     branch = jnp.zeros((positions, channels), F32)
     grad_norm = jnp.zeros((positions, channels), F32)
+    normed_t = normed.T
+    out_parts, in_parts = [], []
     for f in range(hidden // FCHUNK):
         fs = slice(f * FCHUNK, (f + 1) * FCHUNK)
         w_in = w_in_ref[:, fs]
@@ -287,11 +339,13 @@
         per = FCHUNK // out_rows
         for q in range(per):
             out_bufs[0][scat_out.place(f * per + q)] = part[q * out_rows : (q + 1) * out_rows]
-        part = mm(normed, grad_pre, ((0,), (0,))).astype(BF)
+        part = mm(normed_t, grad_pre).astype(BF)
         for q in range(n):
             in_bufs[0][scat_in.place(q), :, fs] = part[q * in_rows : (q + 1) * in_rows]
-    scat_out.start(0)
-    scat_in.start(0)
+        out_parts.append(scat_out.part(f, (out0_s, out0_r), (pl.ds(f * per // 2, per // 2),)))
+        in_parts.append(scat_in.part(f, (in0_s, in0_r), (pl.ds(0, n // 2), slice(None), fs)))
+        out_parts[-1].start()
+        in_parts[-1].start()
 
     standard = std_ref[...]
     grad_std = grad_norm * gain
@@ -317,6 +371,9 @@
     @pl.when(has_dn)
     def _():
         grad_dn().start()
+
+    scat_out.finish_parts(out_parts)
+    scat_in.finish_parts(in_parts)
 
     scale_sum = jnp.zeros((1, channels), F32)
     for a in range(rows):
@@ -331,15 +388,10 @@
     stores[0].start()
     gain_sum = jnp.sum(grad_norm * standard, axis=0, keepdims=True)
 
-    scat_out.finish(0, None)
-    scat_in.finish(0, None)
-
     for h in range(rows):
         line = grad_conv[h * TILE_COLS : (h + 1) * TILE_COLS]
         for j in range(KERNEL):
-            gshift[j, h] = mm(
-                shift_f[:, j * WIN : (j + 1) * WIN], line, ((0,), (0,))
-            ).astype(BF)
+            gshift[j, h] = mm(shift_b[j], line).astype(BF)
     kacc[...] = jnp.zeros(kacc.shape, F32)
 
     def kernel_step(c, _):
@@ -464,12 +516,16 @@
 
 
 def copy_out(*refs):
-    sem = refs[-1]
-    copies = [pltpu.make_async_copy(refs[k], refs[5 + k], sem.at[k]) for k in range(5)]
-    for copy in copies:
-        copy.start()
-    for copy in copies:
-        copy.wait()
+    held, in_sem, out_sem = refs[10:15], refs[15], refs[16]
+    reads = [pltpu.make_async_copy(refs[k], held[k], in_sem.at[k]) for k in range(5)]
+    writes = [pltpu.make_async_copy(held[k], refs[5 + k], out_sem.at[k]) for k in range(5)]
+    for read in reads:
+        read.start()
+    for read, write in zip(reads, writes):
+        read.wait()
+        write.start()
+    for write in writes:
+        write.wait()
 
 
 def shards(n, image, tissue, kernel, ln_gain, w_in, w_out, layer_scale, cotangent):
@@ -518,6 +574,8 @@
     scratch += [dma((2,))] * 4 + [dma((bits,))] * 6
     scratch += [vmem(kernel.shape, F32), vmem((1, channels), F32), vmem(w_in.shape, BF),
                 vmem(w_out.shape, BF), vmem((1, channels), F32), vmem(cotangent.shape, BF), dma((7,))]
+    scratch += [dma((hidden // FCHUNK,))] * 4
+    scratch += [vmem((KERNEL, WIN, TILE_COLS), BF), vmem((rows, KERNEL, WIN, channels), F32)]
     scratch += [vmem(r.shape, r.dtype) for r in outputs] + [dma((5,))]
     anywhere = pl.BlockSpec(memory_space=pl.ANY)
     results = pl.pallas_call(
@@ -538,7 +596,7 @@
         out_shape=[jax.ShapeDtypeStruct(r.shape, r.dtype) for r in results],
         in_specs=[anywhere] * 5,
         out_specs=[anywhere] * 5,
-        scratch_shapes=[dma((5,))],
+        scratch_shapes=[vmem(r.shape, r.dtype) for r in results] + [dma((5,))] * 2,
         compiler_params=pltpu.CompilerParams(vmem_limit_bytes=60 * 1024 * 1024),
     )(*results)
 

time: 81.4 us -> 45 us (0.55)
  Pallas kernels: 80.6 us -> 44.2 us
    pallas_call x1, Pallas kernels: 38.6 us -> 2.14 us  [shards(): pl.pallas_call(copy_out, out_shape=[jax.ShapeDtypeStruct(r.shape, r.dtype...]
where the time goes in v3:
time: 45 us; the launch traced here: 44.9 us
  Pallas kernels  44.2 us (98%)
  between operations  0.64 us (1%)
    pallas_call x1, Pallas kernels, shards(): pl.pallas_call(functools.partial(body, n, bits), out_shape=outputs, in_sp...  42.1 us
    pallas_call x1, Pallas kernels, shards(): pl.pallas_call(copy_out, out_shape=[jax.ShapeDtypeStruct(r.shape, r.dtype...  2.14 us

profile of v3, /device:TPU:0, one launch (start us, length us, event | category | flops | bytes accessed | tf_op | source)
XLA Modules:
  0.0 44.9 jit_solution(9024956947864793666)
XLA Ops:
  0.6 42.1 %shard_map.119 = (bf16[4,256,256]{2,1,0:T(8,128)(2,1)}, bf16[4,256,256]{2,1,0:T(8,128)(2,1)}, f32[16,1024]{1,0:T(8,128)}, f32[64,256]{1,0:T(8,128)}, f32[51,256]{1,0:T(8,128)}) custom-call(s32[1,2]{1,0:T(1,128)} %tissue_ref.1, bf16[4,256,256]{2,1,0:T(8,128)(2,1)} %image_ref.1, f32[7,7,256]{2,1,0:T(8,128)} %kernel_hbm.1, f32[1,256]{1,0:T(1,128)} %bitcast.2, ...), custom_call_target="tpu_custom_call" | custom-call | tf_op jit(solution)/shard_map/pallas_call | solution.py:581
  42.8 2.1 %shard_map.120 = (bf16[4,256,256]{2,1,0:T(8,128)(2,1)}, bf16[4,256,256]{2,1,0:T(8,128)(2,1)}, f32[16,1024]{1,0:T(8,128)}, f32[64,256]{1,0:T(8,128)}, f32[51,256]{1,0:T(8,128)}) custom-call(bf16[4,256,256]{2,1,0:T(8,128)(2,1)} %get-tuple-element.10.refs_0_, bf16[4,256,256]{2,1,0:T(8,128)(2,1)} %get-tuple-element.11.refs_1_, ...), custom_call_target="tpu_custom_call" | custom-call | tf_op jit(solution)/shard_map/pallas_call | solution.py:594

commit v4 on v3

--- a/solution.py
+++ b/solution.py
@@ -13,6 +13,7 @@
 PAD = 16
 WIN = 144
 FCHUNK = 256
+BLOCK = 32
 
 EPSILON = 1e-06
 ROOT_TWO_PI = 0.7978845608028654
@@ -108,15 +109,15 @@
     out_hbm, gimg_hbm, gwin_hbm, gwout_hbm, small_hbm,
     *scratch,
 ):
-    (ipad, win, kf, kb, shift_f, place_m, place_c, prods, normed_ref, std_ref, istd_ref, grad_ref,
-     gbuf, gup, gdn, gshift, kacc, sums, sums_in, pown, pup, pdn) = scratch[:22]
-    in_bufs = scratch[22 : 22 + bits]
-    in_rbufs = scratch[22 + bits : 22 + 2 * bits]
-    out_bufs = scratch[22 + 2 * bits : 22 + 3 * bits]
-    out_rbufs = scratch[22 + 3 * bits : 22 + 4 * bits]
-    (hs, hr, gs, gr, in_s, in_r, out_s, out_r, sm_s, sm_r) = scratch[22 + 4 * bits : 22 + 4 * bits + 10]
-
-    kernel_ref, gain_ref, w_in_ref, w_out_ref, scale_ref, cot_ref, load_sem = scratch[22 + 4 * bits + 10 : -12]
+    (z_ref, back_ref, act_ref, pre_ref, branch_ref, ipad, win, kf, kb, shift_f, place_m, place_c, prods, normed_ref, std_ref, istd_ref, grad_ref,
+     gbuf, gup, gdn, gshift, kacc, sums, sums_in, pown, pup, pdn) = scratch[:27]
+    in_bufs = scratch[27 : 27 + bits]
+    in_rbufs = scratch[27 + bits : 27 + 2 * bits]
+    out_bufs = scratch[27 + 2 * bits : 27 + 3 * bits]
+    out_rbufs = scratch[27 + 3 * bits : 27 + 4 * bits]
+    (hs, hr, gs, gr, in_s, in_r, out_s, out_r, sm_s, sm_r) = scratch[27 + 4 * bits : 27 + 4 * bits + 10]
+
+    kernel_ref, gain_ref, w_in_ref, w_out_ref, scale_ref, cot_ref, load_sem = scratch[27 + 4 * bits + 10 : -12]
     out_ref, gimg_ref, gwin_ref, gwout_ref, small_ref, store_sem = scratch[-6:]
     in0_s, in0_r, out0_s, out0_r, shift_b, conv_part = scratch[-12:-6]
     stores = [
@@ -316,25 +317,33 @@
     loads[6].wait()
     normed = normed_ref[...]
     grads = grad_ref[...]
-    branch = jnp.zeros((positions, channels), F32)
-    grad_norm = jnp.zeros((positions, channels), F32)
     normed_t = normed.T
     out_parts, in_parts = [], []
-    for f in range(hidden // FCHUNK):
+    chunks = hidden // FCHUNK
+
+    def forward(f):
         fs = slice(f * FCHUNK, (f + 1) * FCHUNK)
-        w_in = w_in_ref[:, fs]
-        w_out = w_out_ref[fs, :]
-        z = mm(normed, w_in)
-        zz = z * z
-        tangent = jnp.tanh(z * (ROOT_TWO_PI + (ROOT_TWO_PI * CUBIC_TERM) * zz))
-        half_up = 0.5 + 0.5 * tangent
-        act = (z * half_up).astype(BF)
-        slope = half_up + z * (half_up * (1.0 - tangent)) * (
-            ROOT_TWO_PI + (3.0 * ROOT_TWO_PI * CUBIC_TERM) * zz
-        )
-        branch = branch + mm(act, w_out)
-        grad_pre = (mm(grads, w_out, ((1,), (1,))) * slope).astype(BF)
-        grad_norm = grad_norm + mm(grad_pre, w_in, ((1,), (1,)))
+        z_ref[f % 2] = mm(normed, w_in_ref[:, fs])
+        back_ref[f % 2] = mm(grads, w_out_ref[fs, :], ((1,), (1,)))
+
+    forward(0)
+    for f in range(chunks):
+        fs = slice(f * FCHUNK, (f + 1) * FCHUNK)
+        if f + 1 < chunks:
+            forward(f + 1)
+        for m in range(0, positions, BLOCK):
+            z = z_ref[f % 2, m : m + BLOCK]
+            zz = z * z
+            tangent = jnp.tanh(z * (ROOT_TWO_PI + (ROOT_TWO_PI * CUBIC_TERM) * zz))
+            half_up = 0.5 + 0.5 * tangent
+            value = z * half_up
+            slope = half_up + (value * (1.0 - tangent)) * (
+                ROOT_TWO_PI + (3.0 * ROOT_TWO_PI * CUBIC_TERM) * zz
+            )
+            act_ref[m : m + BLOCK, fs] = value.astype(BF)
+            pre_ref[m : m + BLOCK, fs] = (back_ref[f % 2, m : m + BLOCK] * slope).astype(BF)
+        act = act_ref[:, fs]
+        grad_pre = pre_ref[:, fs]
         part = mm(act, grads, ((0,), (0,))).astype(BF)
         per = FCHUNK // out_rows
         for q in range(per):
@@ -347,12 +356,21 @@
         out_parts[-1].start()
         in_parts[-1].start()
 
-    standard = std_ref[...]
-    grad_std = grad_norm * gain
-    mean_g = jnp.mean(grad_std, axis=-1, keepdims=True)
-    mean_s = jnp.mean(grad_std * standard, axis=-1, keepdims=True)
-    grad_conv = (istd_ref[...] * (grad_std - mean_g - standard * mean_s)).astype(BF)
-    gbuf[16 : 16 + positions, :] = grad_conv
+    z_ref[0] = mm(pre_ref[...], w_in_ref[...], ((1,), (1,)))
+    gain_sum = jnp.zeros((8, channels), F32)
+    for m in range(0, positions, BLOCK):
+        span = slice(m, m + BLOCK)
+        standard = std_ref[span, :]
+        grad_norm = z_ref[0, span]
+        grad_std = grad_norm * gain
+        both = grad_norm * standard
+        mean_g = jnp.mean(grad_std, axis=-1, keepdims=True)
+        mean_s = jnp.mean(both * gain, axis=-1, keepdims=True)
+        gbuf[16 + m : 16 + m + BLOCK, :] = (
+            istd_ref[span, :] * (grad_std - mean_g - standard * mean_s)
+        ).astype(BF)
+        gain_sum = gain_sum + jnp.sum(both.reshape(BLOCK // 8, 8, channels), axis=0)
+    gain_sum = jnp.sum(gain_sum, axis=0, keepdims=True)
     flags = jnp.full((16, channels), flag, F32).astype(BF)
     gbuf[0:16, :] = flags
     gbuf[16 + positions :, :] = flags
@@ -375,21 +393,16 @@
     scat_out.finish_parts(out_parts)
     scat_in.finish_parts(in_parts)
 
-    scale_sum = jnp.zeros((1, channels), F32)
+    branch_ref[...] = mm(act_ref[...], w_out_ref[...])
+    scale_sum = jnp.zeros((8, channels), F32)
     for a in range(rows):
-        span = slice(a * TILE_COLS, (a + 1) * TILE_COLS)
         upstream = at_tile(cot_ref, a, TILE_COLS).astype(F32)
-        scale_sum = scale_sum + jnp.sum(branch[span] * upstream, axis=0, keepdims=True)
-        added = scale * branch[span]
-        for s in range(2):
-            weight = flag if s == 1 else 1.0 - flag
-            cs = slice(s * TILE_COLS, (s + 1) * TILE_COLS)
-            out_ref[a, cs, :] = (ipad[HALF + a, PAD + cs.start : PAD + cs.stop, :].astype(F32) + weight * added).astype(BF)
-    stores[0].start()
-    gain_sum = jnp.sum(grad_norm * standard, axis=0, keepdims=True)
+        both = branch_ref[a * TILE_COLS : (a + 1) * TILE_COLS, :] * upstream
+        scale_sum = scale_sum + jnp.sum(both.reshape(TILE_COLS // 8, 8, channels), axis=0)
+    scale_sum = jnp.sum(scale_sum, axis=0, keepdims=True)
 
     for h in range(rows):
-        line = grad_conv[h * TILE_COLS : (h + 1) * TILE_COLS]
+        line = gbuf[16 + h * TILE_COLS : 16 + (h + 1) * TILE_COLS, :]
         for j in range(KERNEL):
             gshift[j, h] = mm(shift_b[j], line).astype(BF)
     kacc[...] = jnp.zeros(kacc.shape, F32)
@@ -418,6 +431,25 @@
         return remote(sums.at[k], sums_in.at[k], sm_s.at[k], sm_r.at[k], other(me, k))
 
     small(0).start()
+
+    def small_next(k):
+        small(k).wait()
+        if k + 1 < bits:
+            sums[k + 1] = sums[k] + sums_in[k]
+            small(k + 1).start()
+        else:
+            small_ref[...] = (sums[k] + sums_in[k])[: small_ref.shape[0]]
+
+    for a in range(rows):
+        for m in range(0, TILE_COLS, BLOCK):
+            added = scale * branch_ref[a * TILE_COLS + m : a * TILE_COLS + m + BLOCK, :]
+            for s in range(2):
+                weight = flag if s == 1 else 1.0 - flag
+                at = s * TILE_COLS + m
+                base = ipad[HALF + a, PAD + at : PAD + at + BLOCK, :].astype(F32)
+                out_ref[a, at : at + BLOCK, :] = (base + weight * added).astype(BF)
+    stores[0].start()
+    small_next(0)
     scat_out.finish(1, None)
     scat_in.finish(1, None)
 
@@ -434,18 +466,6 @@
         return 0
 
     lax.fori_loop(0, TILE_COLS // 16, back_step, 0)
-
-    def small_next(k):
-        small(k).wait()
-        if k + 1 < bits:
-            sums[k + 1] = sums[k] + sums_in[k]
-            small(k + 1).start()
-        else:
-            small_ref[...] = (sums[k] + sums_in[k])[: small_ref.shape[0]]
-
-    small_next(0)
-    scat_out.finish(2, gwout_ref)
-    scat_in.finish(2, gwin_ref)
 
     @pl.when(has_up)
     def _():
@@ -475,6 +495,8 @@
 
     lax.fori_loop(0, TILE_COLS // 16, halo_step, 0)
     small_next(1)
+    scat_out.finish(2, gwout_ref)
+    scat_in.finish(2, gwin_ref)
 
     def placing(value):
         return place_m[...] + place_c[...] * value
@@ -544,6 +566,11 @@
         jax.ShapeDtypeStruct((KERNEL * KERNEL + 2, channels), F32),
     )
     scratch = [
+        vmem((2, positions, FCHUNK), F32),
+        vmem((2, positions, FCHUNK), F32),
+        vmem((positions, hidden), BF),
+        vmem((positions, hidden), BF),
+        vmem((positions, channels), F32),
         vmem((rows + 2 * HALF, cols + 2 * PAD, channels), BF),
         vmem((rows + 2 * HALF, WIN, channels), BF),
         vmem((KERNEL * KERNEL, 8, channels), F32),

time: 45 us -> 41.5 us (0.922)
  Pallas kernels: 44.2 us -> 40.7 us
    pallas_call x1, Pallas kernels: 42.1 us -> 38.6 us  [shards(): pl.pallas_call(functools.partial(body, n, bits), out_shape=outputs, in_sp...]
where the time goes in v4:
time: 41.5 us; the launch traced here: 41.4 us
  Pallas kernels  40.7 us (98%)
  between operations  0.64 us (2%)
    pallas_call x1, Pallas kernels, shards(): pl.pallas_call(functools.partial(body, n, bits), out_shape=outputs, in_sp...  38.6 us
    pallas_call x1, Pallas kernels, shards(): pl.pallas_call(copy_out, out_shape=[jax.ShapeDtypeStruct(r.shape, r.dtype...  2.14 us

profile of v4, /device:TPU:0, one launch (start us, length us, event | category | flops | bytes accessed | tf_op | source)
XLA Modules:
  0.0 41.4 jit_solution(14444731544257416601)
XLA Ops:
  0.6 38.6 %shard_map.119 = (bf16[4,256,256]{2,1,0:T(8,128)(2,1)}, bf16[4,256,256]{2,1,0:T(8,128)(2,1)}, f32[16,1024]{1,0:T(8,128)}, f32[64,256]{1,0:T(8,128)}, f32[51,256]{1,0:T(8,128)}) custom-call(s32[1,2]{1,0:T(1,128)} %tissue_ref.1, bf16[4,256,256]{2,1,0:T(8,128)(2,1)} %image_ref.1, f32[7,7,256]{2,1,0:T(8,128)} %kernel_hbm.1, f32[1,256]{1,0:T(1,128)} %bitcast.2, ...), custom_call_target="tpu_custom_call" | custom-call | tf_op jit(solution)/shard_map/pallas_call | solution.py:608
  39.2 2.1 %shard_map.120 = (bf16[4,256,256]{2,1,0:T(8,128)(2,1)}, bf16[4,256,256]{2,1,0:T(8,128)(2,1)}, f32[16,1024]{1,0:T(8,128)}, f32[64,256]{1,0:T(8,128)}, f32[51,256]{1,0:T(8,128)}) custom-call(bf16[4,256,256]{2,1,0:T(8,128)(2,1)} %get-tuple-element.10.refs_0_, bf16[4,256,256]{2,1,0:T(8,128)(2,1)} %get-tuple-element.11.refs_1_, ...), custom_call_target="tpu_custom_call" | custom-call | tf_op jit(solution)/shard_map/pallas_call | solution.py:621

commit v5 on v4

--- a/solution.py
+++ b/solution.py
@@ -117,9 +117,10 @@
     out_rbufs = scratch[27 + 3 * bits : 27 + 4 * bits]
     (hs, hr, gs, gr, in_s, in_r, out_s, out_r, sm_s, sm_r) = scratch[27 + 4 * bits : 27 + 4 * bits + 10]
 
-    kernel_ref, gain_ref, w_in_ref, w_out_ref, scale_ref, cot_ref, load_sem = scratch[27 + 4 * bits + 10 : -12]
+    kernel_ref, gain_ref, w_in_ref, w_out_ref, scale_ref, cot_ref, load_sem = scratch[27 + 4 * bits + 10 : -17]
     out_ref, gimg_ref, gwin_ref, gwout_ref, small_ref, store_sem = scratch[-6:]
-    in0_s, in0_r, out0_s, out0_r, shift_b, conv_part = scratch[-12:-6]
+    (in0_s, in0_r, out0_s, out0_r, flag_out, flag_in, halo_out, flag_s, flag_r,
+     shift_b, conv_part) = scratch[-17:-6]
     stores = [
         pltpu.make_async_copy(src, dst, store_sem.at[k])
         for k, (src, dst) in enumerate((
@@ -134,7 +135,7 @@
     loads = [
         pltpu.make_async_copy(src, dst, load_sem.at[k])
         for k, (src, dst) in enumerate((
-            (image_ref, ipad.at[HALF : HALF + rows, PAD : PAD + cols]),
+            (image_ref, ipad.at[:, PAD : PAD + cols]),
             (kernel_hbm, kernel_ref), (gain_hbm, gain_ref), (scale_hbm, scale_ref),
             (cot_hbm, cot_ref), (w_in_hbm, w_in_ref), (w_out_hbm, w_out_ref),
         ))
@@ -161,20 +162,26 @@
     def _():
         signal(me + 1)
 
-    ipad[:, 0:PAD, :] = jnp.zeros((rows + 2 * HALF, PAD, channels), BF)
-    ipad[:, PAD + cols :, :] = jnp.zeros((rows + 2 * HALF, PAD, channels), BF)
-    edge_rows = jnp.zeros((HALF, cols, channels), BF)
+    tile = tissue_ref[0, 1]
+    flag = tile.astype(F32)
+    flag_out[...] = jnp.full(flag_out.shape, flag, F32)
+    ipad[:, 0:PAD, :] = jnp.zeros((rows, PAD, channels), BF)
+    ipad[:, PAD + cols :, :] = jnp.zeros((rows, PAD, channels), BF)
+    edge_rows = jnp.zeros((HALF, WIN, channels), BF)
     edge_grad = jnp.zeros(gup.shape, BF)
+    edge_flag = jnp.zeros(flag_out.shape, F32)
 
     @pl.when(me == 0)
     def _():
-        ipad[0:HALF, PAD : PAD + cols, :] = edge_rows
+        win[0:HALF] = edge_rows
         gup[...] = edge_grad
+        flag_in[0] = edge_flag
 
     @pl.when(me == n - 1)
     def _():
-        ipad[HALF + rows :, PAD : PAD + cols, :] = edge_rows
+        win[HALF + rows :] = edge_rows
         gdn[...] = edge_grad
+        flag_in[1] = edge_flag
 
     count = bits + jnp.where(me > 0, 1, 0) + jnp.where(me < n - 1, 1, 0)
     pl.semaphore_wait(pltpu.get_barrier_semaphore(), count)
@@ -185,13 +192,45 @@
             device_id={"row": target}, device_id_type=pl.DeviceIdType.MESH,
         )
 
+    def flag_dn():
+        return remote(flag_out, flag_in.at[0], flag_s.at[0], flag_r.at[0], me + 1)
+
+    def flag_up():
+        return remote(flag_out, flag_in.at[1], flag_s.at[1], flag_r.at[1], me - 1)
+
     def halo_dn():
-        return remote(image_ref.at[rows - HALF : rows], ipad.at[0:HALF, PAD : PAD + cols],
-                      hs.at[0], hr.at[0], me + 1)
+        return remote(halo_out.at[0], win.at[0:HALF], hs.at[0], hr.at[0], me + 1)
 
     def halo_up():
-        return remote(image_ref.at[0:HALF], ipad.at[HALF + rows : rows + 2 * HALF, PAD : PAD + cols],
-                      hs.at[1], hr.at[1], me - 1)
+        return remote(halo_out.at[1], win.at[HALF + rows : rows + 2 * HALF], hs.at[1], hr.at[1], me - 1)
+
+    @pl.when(has_dn)
+    def _():
+        flag_dn().start()
+
+    @pl.when(has_up)
+    def _():
+        flag_up().start()
+
+    select = ones_where((WIN, WIN + PAD), lambda x, y: y == x + PAD - HALF)
+
+    def at_tile(ref, r, width, value):
+        left, right = ref[r, 0:width, :], ref[r, TILE_COLS : TILE_COLS + width, :]
+        right_part = value.astype(BF)
+        return left * (1.0 - value).astype(BF) + right * right_part
+
+    def window(r, value):
+        return mm(select, at_tile(ipad, r, WIN + PAD, value)).astype(BF)
+
+    in_right = jnp.full((1, 1), flag, F32)
+    loads[0].wait()
+
+    @pl.when(has_dn)
+    def _():
+        flag_up().wait_recv()
+
+    for r in range(HALF):
+        halo_out[0, r] = window(rows - HALF + r, flag_in[1, 0:1, 0:1])
 
     @pl.when(has_dn)
     def _():
@@ -199,16 +238,17 @@
 
     @pl.when(has_up)
     def _():
+        flag_dn().wait_recv()
+
+    for r in range(HALF):
+        halo_out[1, r] = window(r, flag_in[0, 0:1, 0:1])
+
+    @pl.when(has_up)
+    def _():
         halo_up().start()
 
-    tile = tissue_ref[0, 1]
-    flag = tile.astype(F32)
-    in_right = jnp.full((1, 1), flag, F32).astype(BF)
-    in_left = jnp.full((1, 1), 1.0 - flag, F32).astype(BF)
-
-    def at_tile(ref, r, width):
-        left, right = ref[r, 0:width, :], ref[r, TILE_COLS : TILE_COLS + width, :]
-        return left * in_left + right * in_right
+    for r in range(rows):
+        win[HALF + r] = window(r, in_right)
 
     loads[1].wait()
     for i in range(KERNEL):
@@ -227,22 +267,14 @@
         place_m[TILE_COLS:, lanes] = left
         place_c[0:TILE_COLS, lanes] = right - low
         place_c[TILE_COLS:, lanes] = low - left
-    select = ones_where((WIN, WIN + PAD), lambda x, y: y == x + PAD - HALF)
     for load in loads[2:5]:
         load.wait()
     scale = scale_ref[...]
     gain = gain_ref[...]
     for a in range(rows):
         span = slice(a * TILE_COLS, (a + 1) * TILE_COLS)
-        upstream = at_tile(cot_ref, a, TILE_COLS).astype(F32)
+        upstream = at_tile(cot_ref, a, TILE_COLS, in_right).astype(F32)
         grad_ref[span, :] = (scale * upstream).astype(BF)
-
-    def window(r):
-        win[r] = mm(select, at_tile(ipad, r, WIN + PAD)).astype(BF)
-
-    loads[0].wait()
-    for r in range(HALF, HALF + rows):
-        window(r)
 
     LANES = (slice(0, 128), slice(128, 256))
 
@@ -269,15 +301,9 @@
     def _():
         halo_dn().wait_recv()
 
-    for r in range(HALF):
-        window(r)
-
     @pl.when(has_dn)
     def _():
         halo_up().wait_recv()
-
-    for r in range(HALF + rows, rows + 2 * HALF):
-        window(r)
 
     def conv_halo(c, _):
         at = pl.ds(pl.multiple_of(c * 16, 16), 16)
@@ -396,7 +422,7 @@
     branch_ref[...] = mm(act_ref[...], w_out_ref[...])
     scale_sum = jnp.zeros((8, channels), F32)
     for a in range(rows):
-        upstream = at_tile(cot_ref, a, TILE_COLS).astype(F32)
+        upstream = at_tile(cot_ref, a, TILE_COLS, in_right).astype(F32)
         both = branch_ref[a * TILE_COLS : (a + 1) * TILE_COLS, :] * upstream
         scale_sum = scale_sum + jnp.sum(both.reshape(TILE_COLS // 8, 8, channels), axis=0)
     scale_sum = jnp.sum(scale_sum, axis=0, keepdims=True)
@@ -446,7 +472,7 @@
             for s in range(2):
                 weight = flag if s == 1 else 1.0 - flag
                 at = s * TILE_COLS + m
-                base = ipad[HALF + a, PAD + at : PAD + at + BLOCK, :].astype(F32)
+                base = ipad[a, PAD + at : PAD + at + BLOCK, :].astype(F32)
                 out_ref[a, at : at + BLOCK, :] = (base + weight * added).astype(BF)
     stores[0].start()
     small_next(0)
@@ -502,7 +528,7 @@
         return place_m[...] + place_c[...] * value
 
     depth = KERNEL * TILE_COLS
-    at_own = placing(in_right)
+    at_own = placing(in_right.astype(BF))
     at_up = placing(gup[reach : reach + 1, 0:1])
     at_dn = placing(gdn[0:1, 0:1])
     for a in range(rows):
@@ -525,11 +551,13 @@
 
     @pl.when(has_dn)
     def _():
+        flag_dn().wait_send()
         halo_dn().wait_send()
         grad_dn().wait_send()
 
     @pl.when(has_up)
     def _():
+        flag_up().wait_send()
         halo_up().wait_send()
         grad_up().wait_send()
 
@@ -571,7 +599,7 @@
         vmem((positions, hidden), BF),
         vmem((positions, hidden), BF),
         vmem((positions, channels), F32),
-        vmem((rows + 2 * HALF, cols + 2 * PAD, channels), BF),
+        vmem((rows, cols + 2 * PAD, channels), BF),
         vmem((rows + 2 * HALF, WIN, channels), BF),
         vmem((KERNEL * KERNEL, 8, channels), F32),
         vmem((KERNEL * KERNEL, 16, channels), BF),
@@ -602,6 +630,8 @@
     scratch += [vmem(kernel.shape, F32), vmem((1, channels), F32), vmem(w_in.shape, BF),
                 vmem(w_out.shape, BF), vmem((1, channels), F32), vmem(cotangent.shape, BF), dma((7,))]
     scratch += [dma((hidden // FCHUNK,))] * 4
+    scratch += [vmem((8, 128), F32), vmem((2, 8, 128), F32), vmem((2, HALF, WIN, channels), BF)]
+    scratch += [dma((2,))] * 2
     scratch += [vmem((KERNEL, WIN, TILE_COLS), BF), vmem((rows, KERNEL, WIN, channels), F32)]
     scratch += [vmem(r.shape, r.dtype) for r in outputs] + [dma((5,))]
     anywhere = pl.BlockSpec(memory_space=pl.ANY)

time: 41.5 us -> 41.1 us (level)
    pallas_call x1, Pallas kernels: 38.6 us -> 38.1 us  [shards(): pl.pallas_call(functools.partial(body, n, bits), out_shape=outputs, in_sp...]
where the time goes in v5:
time: 41.1 us; the launch traced here: 40.9 us
  Pallas kernels  40.3 us (98%)
  between operations  0.64 us (2%)
    pallas_call x1, Pallas kernels, shards(): pl.pallas_call(functools.partial(body, n, bits), out_shape=outputs, in_sp...  38.1 us
    pallas_call x1, Pallas kernels, shards(): pl.pallas_call(copy_out, out_shape=[jax.ShapeDtypeStruct(r.shape, r.dtype...  2.14 us

profile of v5, /device:TPU:0, one launch (start us, length us, event | category | flops | bytes accessed | tf_op | source)
XLA Modules:
  0.0 40.9 jit_solution(523857505727649694)
XLA Ops:
  0.6 38.1 %shard_map.119 = (bf16[4,256,256]{2,1,0:T(8,128)(2,1)}, bf16[4,256,256]{2,1,0:T(8,128)(2,1)}, f32[16,1024]{1,0:T(8,128)}, f32[64,256]{1,0:T(8,128)}, f32[51,256]{1,0:T(8,128)}) custom-call(s32[1,2]{1,0:T(1,128)} %tissue_ref.1, bf16[4,256,256]{2,1,0:T(8,128)(2,1)} %image_ref.1, f32[7,7,256]{2,1,0:T(8,128)} %kernel_hbm.1, f32[1,256]{1,0:T(1,128)} %bitcast.2, ...), custom_call_target="tpu_custom_call" | custom-call | tf_op jit(solution)/shard_map/pallas_call | solution.py:638
  38.8 2.1 %shard_map.120 = (bf16[4,256,256]{2,1,0:T(8,128)(2,1)}, bf16[4,256,256]{2,1,0:T(8,128)(2,1)}, f32[16,1024]{1,0:T(8,128)}, f32[64,256]{1,0:T(8,128)}, f32[51,256]{1,0:T(8,128)}) custom-call(bf16[4,256,256]{2,1,0:T(8,128)(2,1)} %get-tuple-element.10.refs_0_, bf16[4,256,256]{2,1,0:T(8,128)(2,1)} %get-tuple-element.11.refs_1_, ...), custom_call_target="tpu_custom_call" | custom-call | tf_op jit(solution)/shard_map/pallas_call | solution.py:651
